TPU v7x, 32 devices: a whole 2x2x4 slice. The times are simulated.
32 devices in a mesh: sky: 8 (over z, x), src: 4 (over y, core).
Axes of the slice: x: 2, y: 2, z: 4, core: 2. Of those that a mesh axis runs over, the one named last changes fastest.
Arguments:
- exposures: float32 [8, 64, 256, 256], P('sky', 'src'), may hold values from -6 to 6
- variance: float32 [8, 64, 256, 256], P('sky', 'src'), may hold values from 0.25 to 4
- coef_table: float32 [64, 45], replicated, may hold values from -6 to 6
- coef_index: int32 [8, 64], P('sky', 'src'), may hold values from 0 to 63
- offsets: int32 [8, 64, 2], P('sky', 'src'), may hold values from 0 to 256
- tile_codes: int32 [8, 64], P('sky', 'src'), may hold values from 0 to 7, as said below
- detect_ra: float32 [41], replicated, may hold values from -1 to 1
- detect_dec: float32 [41], replicated, may hold values from -1 to 1
Outputs:
- coadd: float32 [4096, 2048], P('sky', 'src')
- detection: float32 [4096, 2048], P('sky', 'src')
Inputs may be any that keep to these rules, and one draw needn't show every extreme that they name: `tile_codes`: code c sends a tile to the patch row c // 4 after the holder's own (wrapping around) and to owner c mod 4 along src. On one device at most 2 tiles name the same code; in every sky row one code is named by exactly 2 tiles on every device of that row.
All inputs are finite; a program needn't handle non-finite values.
Results may differ from a plain program's by a relative error of at most 0.0003.
Values sent between devices are 32-bit elements; how exact they have to be, the bound alone decides.
A program may use at most 192 MiB of HBM per device.

v0:
```python
import functools

import ml_dtypes
import numpy as np
import jax
import jax.numpy as jnp
from jax import lax
from jax.experimental import pallas as pl
from jax.experimental.pallas import tpu as pltpu
from jax.sharding import PartitionSpec as P

CAP = 2
KSIZE = 21
SPREADS = (0.75, 1.5, 3.0)
LANES = 128
LEAD = 16
ROWS = 64
VMEM = 60 * 2**20
HIGHEST = lax.Precision.HIGHEST


def halves(value):
    high = value.astype(jnp.bfloat16)
    return high, (value - high.astype(jnp.float32)).astype(jnp.bfloat16)


def product_of(left, right):
    dot = functools.partial(jnp.dot, preferred_element_type=jnp.float32)
    return dot(left[1], right[0]) + dot(left[0], right[1]) + dot(left[0], right[0])


def basis_filters():
    centred = np.arange(KSIZE, dtype=np.float64) - KSIZE // 2
    along_x, along_y = [], []
    for spread in SPREADS:
        gaussian = np.exp(-(centred * centred) / (2.0 * spread * spread))
        scaled = centred / spread
        for power_x in range(5):
            for power_y in range(5 - power_x):
                filter_x = gaussian * scaled**power_x
                filter_y = gaussian * scaled**power_y
                along_x.append(filter_x / np.sum(np.abs(filter_x)))
                along_y.append(filter_y / np.sum(np.abs(filter_y)))
    return np.stack(along_y), np.stack(along_x)


def transforms(extent):
    radius = KSIZE // 2
    length = extent + 2 * radius
    main = extent // 2
    low = np.arange(main)
    high = np.arange(main, length // 2 + 1)
    extra = high.size
    step = 2.0 * np.pi / length

    def trig(points, freqs):
        angle = step * np.outer(points, freqs)
        return np.cos(angle), np.sin(angle)

    def packed(first, second):
        out = np.zeros((first.shape[0], LANES))
        out[:, :extra] = first
        out[:, extra : 2 * extra] = second
        return out

    pixels = np.arange(extent)
    taps = np.arange(KSIZE) - radius
    cos_low, sin_low = trig(pixels, low)
    cos_high, sin_high = trig(pixels, high)
    forward = np.concatenate(
        [cos_low, sin_low, packed(cos_high, sin_high), packed(sin_high, cos_high)], 1
    )
    gain_low = np.where(low == 0, 1.0, 2.0) / length
    gain_high = np.where(high == length // 2, 1.0, 2.0) / length
    inverse = np.concatenate(
        [cos_low * gain_low, sin_low * gain_low, packed(cos_high * gain_high, sin_high * gain_high)],
        1,
    ).T
    tap_cos_low, tap_sin_low = trig(taps, low)
    tap_cos_high, tap_sin_high = trig(taps, high)
    tap_lanes = np.concatenate(
        [
            tap_cos_low,
            tap_sin_low,
            packed(tap_cos_high, tap_cos_high),
            packed(tap_sin_high, -tap_sin_high),
        ],
        1,
    )
    def split(matrix):
        high = matrix.astype(ml_dtypes.bfloat16)
        return np.stack([high, (matrix - high.astype(np.float64)).astype(ml_dtypes.bfloat16)])

    return split(forward), split(inverse), tap_lanes


def place_kernel(
    patch,
    pick,
    coef,
    corner,
    fill,
    exp_ref,
    var_ref,
    table_ref,
    forward_ref,
    inverse_ref,
    numer_in,
    denom_in,
    numer_out,
    denom_out,
    spectrum,
    product,
    numer_acc,
    denom_acc,
):
    step = pl.program_id(0)
    extent = exp_ref.shape[-1]
    groups = spectrum.shape[0]
    half = (groups - 2) // 2
    radius = KSIZE // 2

    @pl.when(step == 0)
    def _():
        numer_acc[:patch, :] = numer_in[...]
        denom_acc[:patch, :] = denom_in[...]
        blank = jnp.zeros((8, patch), jnp.float32)
        numer_acc[patch:, :] = blank
        denom_acc[patch:, :] = blank
        edge = jnp.zeros((groups, LEAD, LANES), jnp.float32)
        spectrum[:, :LEAD, :] = edge
        spectrum[:, LEAD + extent :, :] = edge

    lines = product_of(halves(exp_ref[0, 0]), (forward_ref[0], forward_ref[1]))
    for group in range(groups):
        spectrum[group, LEAD : LEAD + extent, :] = lines[:, group * LANES : (group + 1) * LANES]

    def taps_of(tap, group):
        return table_ref[0, tap : tap + 1, group * LANES : (group + 1) * LANES]

    for base in range(0, extent, ROWS):
        for group in range(half):
            real = jnp.zeros((ROWS, LANES), jnp.float32)
            imag = jnp.zeros((ROWS, LANES), jnp.float32)
            for tap in range(KSIZE):
                at = base + tap + LEAD - radius
                cosine = spectrum[group, at : at + ROWS, :]
                sine = spectrum[half + group, at : at + ROWS, :]
                tap_cos = taps_of(tap, group)
                tap_sin = taps_of(tap, half + group)
                real = real + tap_cos * cosine + tap_sin * sine
                imag = imag + tap_cos * sine - tap_sin * cosine
            product[base : base + ROWS, group * LANES : (group + 1) * LANES] = real
            product[
                base : base + ROWS, (half + group) * LANES : (half + group + 1) * LANES
            ] = imag
        both = jnp.zeros((ROWS, LANES), jnp.float32)
        for tap in range(KSIZE):
            at = base + tap + LEAD - radius
            both = (
                both
                + taps_of(tap, groups - 2) * spectrum[groups - 2, at : at + ROWS, :]
                + taps_of(tap, groups - 1) * spectrum[groups - 1, at : at + ROWS, :]
            )
        product[base : base + ROWS, (groups - 2) * LANES :] = both

    matched = product_of(halves(product[...]), (inverse_ref[0], inverse_ref[1]))
    weight = fill[step].astype(jnp.float32) / var_ref[0, 0]
    row, col = corner[2 * step], corner[2 * step + 1]
    low_row = lax.rem(row, 8)
    first = pl.multiple_of(row - low_row, 8)

    def placed(tile):
        wide = jnp.concatenate([tile, jnp.zeros((extent, patch - extent), jnp.float32)], 1)
        wide = pltpu.roll(wide, col, 1)
        wide = jnp.concatenate([wide, jnp.zeros((8, patch), jnp.float32)], 0)
        return pltpu.roll(wide, low_row, 0)

    where = pl.ds(first, extent + 8)
    numer_acc[where, :] = numer_acc[where, :] + placed(weight * matched)
    denom_acc[where, :] = denom_acc[where, :] + placed(weight)

    @pl.when(step == pl.num_programs(0) - 1)
    def _():
        numer_out[...] = numer_acc[:patch, :]
        denom_out[...] = denom_acc[:patch, :]


def place_tiles(canvases, tiles, variance, plane, pick, about, tables, forward, inverse):
    coef, corner, fill = about
    patch = canvases[0].shape[0]
    extent = tiles.shape[-1]
    lanes = forward.shape[-1]
    count = pick.shape[0]

    def whole(*shape):
        return pl.BlockSpec(shape, lambda i, *refs: (0,) * len(shape))

    def tile_spec(which):
        return pl.BlockSpec(
            (1, 1, extent, extent), lambda i, pick, *refs: (which, pick[i], 0, 0)
        )

    grid_spec = pltpu.PrefetchScalarGridSpec(
        num_scalar_prefetch=4,
        grid=(count,),
        in_specs=[
            tile_spec(0),
            tile_spec(plane),
            pl.BlockSpec((1, KSIZE, lanes), lambda i, pick, coef, *refs: (coef[i], 0, 0)),
            whole(*forward.shape),
            whole(*inverse.shape),
            whole(patch, patch),
            whole(patch, patch),
        ],
        out_specs=[whole(patch, patch), whole(patch, patch)],
        scratch_shapes=[
            pltpu.VMEM((lanes // LANES, extent + 2 * LEAD, LANES), jnp.float32),
            pltpu.VMEM((extent, lanes - LANES), jnp.float32),
            pltpu.VMEM((patch + 8, patch), jnp.float32),
            pltpu.VMEM((patch + 8, patch), jnp.float32),
        ],
    )
    return pl.pallas_call(
        functools.partial(place_kernel, patch),
        grid_spec=grid_spec,
        out_shape=[jax.ShapeDtypeStruct((patch, patch), jnp.float32)] * 2,
        compiler_params=pltpu.CompilerParams(
            vmem_limit_bytes=VMEM
        ),
        cost_estimate=pl.CostEstimate(
            flops=count * 80 * extent * extent * lanes,
            bytes_accessed=16 * patch * patch + count * 8 * extent * extent,
            transcendentals=0,
        ),
    )(pick, coef, corner.reshape(-1), fill, tiles, variance, tables, forward, inverse, *canvases)


def gather_kernel(pick, exp_ref, var_ref, out_ref):
    out_ref[0] = exp_ref[...]
    out_ref[1] = var_ref[...]


def gather_tiles(tiles, variance, pick):
    extent = tiles.shape[-1]
    count = pick.shape[0]
    tile_spec = pl.BlockSpec((1, extent, extent), lambda i, pick: (pick[i], 0, 0))
    return pl.pallas_call(
        gather_kernel,
        grid_spec=pltpu.PrefetchScalarGridSpec(
            num_scalar_prefetch=1,
            grid=(count,),
            in_specs=[tile_spec, tile_spec],
            out_specs=pl.BlockSpec((2, 1, extent, extent), lambda i, pick: (0, i, 0, 0)),
        ),
        out_shape=jax.ShapeDtypeStruct((2, count, extent, extent), jnp.float32),
        compiler_params=pltpu.CompilerParams(vmem_limit_bytes=VMEM),
        cost_estimate=pl.CostEstimate(
            flops=0, bytes_accessed=16 * count * extent * extent, transcendentals=0
        ),
    )(pick, tiles, variance)


def band(taps, outputs):
    size = taps.shape[0]
    shape = (outputs + size - 1, outputs)
    lag = lax.broadcasted_iota(jnp.int32, shape, 0) - lax.broadcasted_iota(jnp.int32, shape, 1)
    out = jnp.zeros(shape, jnp.float32)
    for tap in range(size):
        out = jnp.where(lag == tap, taps[tap], out)
    return out


def inner_and_rims(matrix, rim, axis):
    size = matrix.shape[axis]
    cut = functools.partial(lax.slice_in_dim, matrix, axis=axis)
    return cut(rim, size - rim), jnp.concatenate([cut(0, rim), cut(size - rim, size)], axis)


def columns_kernel(rows_ref, edge_ref, middle_ref, edges_ref, out_ref):
    out_ref[...] = product_of(halves(rows_ref[...]), halves(middle_ref[...])) + product_of(
        halves(edge_ref[...]), halves(edges_ref[...])
    )


def rows_kernel(
    filtered_ref, near_ref, corner_ref, middle_ref, edges_ref, across_ref, rims_ref, out_ref
):
    outside = product_of(halves(near_ref[...]), halves(middle_ref[...])) + product_of(
        halves(corner_ref[...]), halves(edges_ref[...])
    )
    out_ref[...] = product_of(halves(across_ref[...]), halves(filtered_ref[...])) + product_of(
        halves(rims_ref[...]), halves(outside)
    )


def filter_call(kernel, *operands):
    return pl.pallas_call(
        kernel,
        out_shape=jax.ShapeDtypeStruct(operands[0].shape, jnp.float32),
        in_specs=[pl.BlockSpec(memory_space=pltpu.VMEM)] * len(operands),
        out_specs=pl.BlockSpec(memory_space=pltpu.VMEM),
        compiler_params=pltpu.CompilerParams(vmem_limit_bytes=VMEM),
        cost_estimate=pl.CostEstimate(
            flops=6 * operands[0].size * operands[0].shape[1],
            bytes_accessed=sum(4 * operand.size for operand in operands),
            transcendentals=0,
        ),
    )(*operands)


filter_columns = functools.partial(filter_call, columns_kernel)
filter_rows = functools.partial(filter_call, rows_kernel)


def shifted(value, sky_step, src_step):
    skies, owners = lax.axis_size("sky"), lax.axis_size("src")
    pairs = []
    for sky in range(skies):
        for src in range(owners):
            to = src + src_step
            if 0 <= to < owners:
                target = ((sky + sky_step) % skies) * owners + to
                pairs.append((sky * owners + src, target))
    return lax.ppermute(value, ("sky", "src"), pairs)


def on_device(
    exposures, variance, coef_table, coef_index, offsets, tile_codes, detect_ra, detect_dec
):
    owners = lax.axis_size("src")
    me = lax.axis_index("src")
    tiles, variances = exposures[0], variance[0]
    count, extent = tiles.shape[0], tiles.shape[-1]
    patch = 2 * extent
    codes_here = tile_codes[0]
    entries = jnp.arange(count, dtype=jnp.int32)

    same = codes_here[:, None] == codes_here[None, :]
    earlier = entries[None, :] < entries[:, None]
    rank = jnp.sum((same & earlier).astype(jnp.int32), -1)

    slot = jnp.arange(2 * owners * CAP, dtype=jnp.int32).reshape(2 * owners, CAP, 1)
    chooser = (codes_here * CAP + rank == slot).astype(jnp.int32)
    source = jnp.sum(chooser * entries, -1).reshape(2, owners, CAP)

    about = jnp.concatenate([coef_index[0][:, None], offsets[0]], 1)
    notes = jnp.sum(chooser[..., None] * about, 2)
    notes = jnp.concatenate([notes, jnp.sum(chooser, -1)[..., None]], -1)
    notes = notes.reshape(2, owners, CAP, 4)

    forward, inverse, tap_lanes = transforms(extent)
    along_y, along_x = basis_filters()
    lanes_x = (along_x @ tap_lanes).astype(np.float32)
    basis = jnp.asarray(along_y.astype(np.float32))[:, :, None] * jnp.asarray(lanes_x)[:, None, :]
    tables = jnp.einsum(
        "ck,ksl->csl", coef_table, basis, precision=HIGHEST, preferred_element_type=jnp.float32
    )
    forward, inverse = jnp.asarray(forward), jnp.asarray(inverse)

    def swapped(value, partner):
        return lax.ppermute(value, "src", [(i, i ^ partner) for i in range(owners)])

    def towards(value, partner, axis=0):
        return lax.dynamic_index_in_dim(value, me ^ partner, axis, keepdims=False)

    told = {partner: swapped(towards(notes, partner, 1), partner) for partner in range(1, owners)}
    told[0] = towards(notes, 0, 1)

    def send(row_step, partner, after):
        picks = towards(source[row_step], partner)
        out = gather_tiles(tiles, variances, picks)
        if after is not None:
            out, after = lax.optimization_barrier((out, after))
        return swapped(out, partner), after

    def add(canvases, row_step, partner, held):
        if held is None:
            picks = towards(source[row_step], 0)
            held, spread, plane = tiles[None], variances[None], 0
        else:
            spread, plane = held, 1
            picks = jnp.arange(CAP, dtype=jnp.int32)
        note = told[partner][row_step]
        note = (note[:, 0], note[:, 1:3], note[:, 3])
        return place_tiles(
            canvases, held, spread, plane, picks, note, tables, forward, inverse
        )

    zero = jnp.zeros((patch, patch), jnp.float32)
    far = range(2, owners)
    arrived = {}
    for partner in far:
        arrived[1, partner], _ = send(1, partner, None)
    arrived[1, 1], _ = send(1, 1, None)
    arrived[0, 1], _ = send(0, 1, None)
    for partner in far:
        arrived[0, partner], arrived[1, partner] = send(0, partner, arrived[1, partner])

    ahead = (zero, zero)
    ahead = add(ahead, 1, 0, None)
    ahead = add(ahead, 1, 1, arrived[1, 1])
    here = add((zero, zero), 0, 0, None)
    here = add(here, 0, 1, arrived[0, 1])
    ahead, here = lax.optimization_barrier((ahead, here))
    for partner in far:
        ahead = add(ahead, 1, partner, arrived[1, partner])
    moved = [shifted(value, 1, 0) for value in ahead]
    for partner in far:
        here = add(here, 0, partner, arrived[0, partner])
    coadd = (here[0] + moved[0]) / (here[1] + moved[1] + 1.0)

    rim = detect_ra.shape[0] // 2
    along_dec = band(detect_dec, patch)
    along_ra = band(detect_ra, patch).T
    left = shifted(coadd[:, patch - rim :], 0, 1)
    right = shifted(coadd[:, :rim], 0, -1)

    def rows(first):
        return jnp.concatenate([part[first : first + rim] for part in (coadd, left, right)], 1)

    near = jnp.concatenate([shifted(rows(patch - rim), 1, 0), shifted(rows(0), -1, 0)], 0)
    middle, edges = inner_and_rims(along_dec, rim, 0)
    filtered = filter_columns(coadd, jnp.concatenate([left, right], 1), middle, edges)
    detection = filter_rows(
        filtered,
        near[:, :patch],
        near[:, patch:],
        middle,
        edges,
        *inner_and_rims(along_ra, rim, 1),
    )
    return (coadd, detection)


def solution(mesh):
    return jax.shard_map(
        on_device,
        mesh=mesh,
        in_specs=(
            P("sky", "src", None, None),
            P("sky", "src", None, None),
            P(),
            P("sky", "src"),
            P("sky", "src", None),
            P("sky", "src"),
            P(),
            P(),
        ),
        out_specs=(P("sky", "src"), P("sky", "src")),
        check_vma=False,
    )
```

profile of v0, /device:TPU:1, one launch (start us, length us, event | category | flops | bytes accessed | tf_op | source)
XLA Modules:
  0.0 264.4 jit_solution(15333580687144386836)
XLA Ops:
  3.4 2.9 %shard_map.138 = f32[2,2,256,256]{3,2,1,0:T(8,128)} custom-call(s32[2]{0:T(128)} %get-tuple-element.185.pick, f32[16,256,256]{2,1,0:T(8,128)} %bitcast.115, f32[16,256,256]{2,1,0:T(8,128)} %bitcast.121), custom_call_target="tpu_custom_call" | custom-call | bytes 2097152 | tf_op jit(solution)/shard_map/pallas_call | solution.py:248
  7.5 2.8 %shard_map.135 = f32[2,2,256,256]{3,2,1,0:T(8,128)} custom-call(s32[2]{0:T(128)} %get-tuple-element.67.pick, f32[16,256,256]{2,1,0:T(8,128)} %bitcast.116, f32[16,256,256]{2,1,0:T(8,128)} %bitcast.122), custom_call_target="tpu_custom_call" | custom-call | bytes 2097152 | tf_op jit(solution)/shard_map/pallas_call | solution.py:248
  10.3 2.9 %shard_map.134 = f32[2,2,256,256]{3,2,1,0:T(8,128)} custom-call(s32[2]{0:T(128)} %get-tuple-element.68.pick, f32[16,256,256]{2,1,0:T(8,128)} %bitcast.117, f32[16,256,256]{2,1,0:T(8,128)} %bitcast.123), custom_call_target="tpu_custom_call" | custom-call | bytes 2097152 | tf_op jit(solution)/shard_map/pallas_call | solution.py:248
  13.2 2.7 %collective-permute-start.4 = (f32[2,2,256,256]{3,2,1,0:T(8,128)}, f32[2,2,256,256]{3,2,1,0:T(8,128)}, u32[]{:S(2)}, u32[]{:S(2)}) collective-permute-start(f32[2,2,256,256]{3,2,1,0:T(8,128)} %shard_map.134), channel_id=1, source_target_pairs={{0,2},{1,3},{2,0},{3,1},{4,6},{5,7},{6,4},{7,5},{8,10},{9,11},{10,... | collective-permute-start | bytes 3145736 | tf_op jit(solution)/shard_map/ppermute | solution.py:362
  19.2 26.0 %select_select_fusion.1 = f32[552,512]{1,0:T(8,128)S(1)} fusion(f32[]{:T(128)} %bitcast.58, f32[]{:T(128)} %bitcast.57, f32[]{:T(128)} %bitcast.56, f32[]{:T(128)} %bitcast.55, f32[]{:T(128)} %bitcast.54, f32[]{:T(128)} %bitcast.53, f32[]{:T(128)} %bitcast.52, f32[]{:T(128)} %bitcast.51, f32[]{:T(128)} %bitcast.50, f32[]{:T(128)} %bitcast.49, f32[]{:T(128)} %bitcast.48, ...), kind=kLoop, calls=%fused_computation.46 | loop fusion | flops 23457792 | bytes 1130660 | tf_op jit(solution)/shard_map/jit(_where)/select_n | solution.py:270
  48.5 26.0 %select_select_fusion = f32[512,552]{1,0:T(8,128)S(1)} fusion(f32[]{:T(128)} %bitcast.99, f32[]{:T(128)} %bitcast.98, f32[]{:T(128)} %bitcast.97, f32[]{:T(128)} %bitcast.96, f32[]{:T(128)} %bitcast.95, f32[]{:T(128)} %bitcast.94, f32[]{:T(128)} %bitcast.93, f32[]{:T(128)} %bitcast.92, f32[]{:T(128)} %bitcast.91, f32[]{:T(128)} %bitcast.90, f32[]{:T(128)} %bitcast.89, ...), kind=kLoop, calls=%fused_computation.3 | loop fusion | flops 23457792 | bytes 1130660 | tf_op jit(solution)/shard_map/jit(_where)/select_n | solution.py:270
  76.5 2.9 %fusion = f32[21,512,64]{1,2,0:T(8,128)S(1)} fusion(f32[45,512]{1,0:T(8,128)S(1)} %copy-done.7, f32[45,21]{0,1:T(8,128)S(1)} %copy-done.8, f32[64,45]{0,1:T(8,128)S(1)} %copy-done), kind=kOutput, calls=%fused_computation.1 | convolution fusion | flops 372072960 | bytes 2859972 | tf_op jit(solution)/shard_map/ck,ksl->csl/dot_general | solution.py:356
  79.4 3.3 %copy.56 = f32[21,512,64]{1,0,2:T(8,128)} copy(f32[21,512,64]{1,2,0:T(8,128)S(1)} %fusion) | data formatting | bytes 5505024 | tf_op jit(solution)/shard_map/ck,ksl->csl/dot_general | solution.py:356
  83.4 2.7 %shard_map.133 = f32[2,2,256,256]{3,2,1,0:T(8,128)} custom-call(s32[2]{0:T(128)} %get-tuple-element.184.pick, f32[16,256,256]{2,1,0:T(8,128)} %bitcast.118, f32[16,256,256]{2,1,0:T(8,128)} %bitcast.124), custom_call_target="tpu_custom_call" | custom-call | bytes 2097152 | tf_op jit(solution)/shard_map/pallas_call | solution.py:248
  86.1 2.7 %shard_map.132 = f32[2,2,256,256]{3,2,1,0:T(8,128)} custom-call(s32[2]{0:T(128)} %get-tuple-element.69.pick, f32[16,256,256]{2,1,0:T(8,128)} %bitcast.119, f32[16,256,256]{2,1,0:T(8,128)} %bitcast.125), custom_call_target="tpu_custom_call" | custom-call | bytes 2097152 | tf_op jit(solution)/shard_map/pallas_call | solution.py:248
  88.8 2.7 %shard_map.131 = f32[2,2,256,256]{3,2,1,0:T(8,128)} custom-call(s32[2]{0:T(128)} %get-tuple-element.183.pick, f32[16,256,256]{2,1,0:T(8,128)} %bitcast.120, f32[16,256,256]{2,1,0:T(8,128)} %bitcast.126), custom_call_target="tpu_custom_call" | custom-call | bytes 2097152 | tf_op jit(solution)/shard_map/pallas_call | solution.py:248
  94.1 9.5 %shard_map.139 = (f32[512,512]{1,0:T(8,128)}, f32[512,512]{1,0:T(8,128)}) custom-call(s32[2]{0:T(128)} %get-tuple-element.186.pick, s32[2]{0:T(128)} %get-tuple-element.57.coef, s32[4]{0:T(128)} %reshape.84.corner, s32[2]{0:T(128)} %get-tuple-element.56.fill, f32[1,16,256,256]{3,2,1,0:T(8,128)} %exp_ref.3, f32[1,16,256,256]{3,2,1,0:T(8,128)} %var_ref.3, ...), custom_call_target="tpu_custom_call" | custom-call | flops 5368709120 | bytes 5242880 | tf_op jit(solution)/shard_map/pallas_call | solution.py:224
  103.6 9.8 %shard_map.136 = (f32[512,512]{1,0:T(8,128)}, f32[512,512]{1,0:T(8,128)}) custom-call(s32[2]{0:T(128)} %get-tuple-element.66.pick, s32[2]{0:T(128)} %get-tuple-element.187.coef, s32[4]{0:T(128)} %reshape.82.corner, s32[2]{0:T(128)} %get-tuple-element.188.fill, f32[1,16,256,256]{3,2,1,0:T(8,128)} %exp_ref.3, f32[1,16,256,256]{3,2,1,0:T(8,128)} %var_ref.3, ...), custom_call_target="tpu_custom_call" | custom-call | flops 5368709120 | bytes 5242880 | tf_op jit(solution)/shard_map/pallas_call | solution.py:224
  113.5 1.9 collective-permute-start.1
  117.8 21.0 %collective-permute-done = s32[2,2,4]{2,1,0:T(2,128)S(1)} collective-permute-done((s32[2,2,4]{2,1,0:T(2,128)S(1)}, s32[2,2,4]{2,1,0:T(2,128)S(1)}, u32[]{:S(2)}, u32[]{:S(2)}) %collective-permute-start) | collective-permute-done | bytes 96 | tf_op jit(solution)/shard_map/ppermute | solution.py:362
  144.1 9.5 %shard_map.140 = (f32[512,512]{1,0:T(8,128)}, f32[512,512]{1,0:T(8,128)}) custom-call(s32[2]{0:T(128)} %iota.382.pick, s32[2]{0:T(128)} %get-tuple-element.63.coef, s32[4]{0:T(128)} %reshape.83.corner, s32[2]{0:T(128)} %get-tuple-element.62.fill, f32[2,2,256,256]{3,2,1,0:T(8,128)} %copy-done.11, f32[2,2,256,256]{3,2,1,0:T(8,128)} %copy-done.11, ...), custom_call_target="tpu_custom_call" | custom-call | flops 5368709120 | bytes 5242880 | tf_op jit(solution)/shard_map/pallas_call | solution.py:224
  154.1 9.6 %shard_map.137 = (f32[512,512]{1,0:T(8,128)}, f32[512,512]{1,0:T(8,128)}) custom-call(s32[2]{0:T(128)} %iota.381.pick, s32[2]{0:T(128)} %get-tuple-element.71.coef, s32[4]{0:T(128)} %reshape.81.corner, s32[2]{0:T(128)} %get-tuple-element.70.fill, f32[2,2,256,256]{3,2,1,0:T(8,128)} %collective-permute-done.7.exp_ref.var_ref, ...), custom_call_target="tpu_custom_call" | custom-call | flops 5368709120 | bytes 5242880 | tf_op jit(solution)/shard_map/pallas_call | solution.py:224
  163.7 1.9 collective-permute-start.5
  166.5 9.4 %shard_map.143 = (f32[512,512]{1,0:T(8,128)}, f32[512,512]{1,0:T(8,128)}) custom-call(s32[2]{0:T(128)} %iota.384.pick, s32[2]{0:T(128)} %get-tuple-element.53.coef, s32[4]{0:T(128)} %reshape.86.corner, s32[2]{0:T(128)} %get-tuple-element.52.fill, f32[2,2,256,256]{3,2,1,0:T(8,128)} %collective-permute-done.4.exp_ref.var_ref, ...), custom_call_target="tpu_custom_call" | custom-call | flops 5368709120 | bytes 5242880 | tf_op jit(solution)/shard_map/pallas_call | solution.py:224
  176.5 9.7 %shard_map.144 = (f32[512,512]{1,0:T(8,128)}, f32[512,512]{1,0:T(8,128)}) custom-call(s32[2]{0:T(128)} %iota.383.pick, s32[2]{0:T(128)} %get-tuple-element.55.coef, s32[4]{0:T(128)} %reshape.85.corner, s32[2]{0:T(128)} %get-tuple-element.54.fill, f32[2,2,256,256]{3,2,1,0:T(8,128)} %collective-permute-done.1.exp_ref.var_ref, ...), custom_call_target="tpu_custom_call" | custom-call | flops 5368709120 | bytes 5242880 | tf_op jit(solution)/shard_map/pallas_call | solution.py:224
  186.2 1.7 collective-permute-start.10
  191.8 9.4 %shard_map.141 = (f32[512,512]{1,0:T(8,128)}, f32[512,512]{1,0:T(8,128)}) custom-call(s32[2]{0:T(128)} %iota.380.pick, s32[2]{0:T(128)} %get-tuple-element.73.coef, s32[4]{0:T(128)} %reshape.80.corner, s32[2]{0:T(128)} %get-tuple-element.72.fill, f32[2,2,256,256]{3,2,1,0:T(8,128)} %collective-permute-done.5.exp_ref.var_ref, ...), custom_call_target="tpu_custom_call" | custom-call | flops 5368709120 | bytes 5242880 | tf_op jit(solution)/shard_map/pallas_call | solution.py:224
  201.3 10.5 %collective-permute-done.2.exp_ref.var_ref = f32[2,2,256,256]{3,2,1,0:T(8,128)} collective-permute-done((f32[2,2,256,256]{3,2,1,0:T(8,128)S(1)}, f32[2,2,256,256]{3,2,1,0:T(8,128)}, u32[]{:S(2)}, u32[]{:S(2)}) %collective-permute-start.2) | collective-permute-done | bytes 1048608 | tf_op jit(solution)/shard_map/ppermute | solution.py:362
  212.3 9.5 %shard_map.142 = (f32[512,512]{1,0:T(8,128)}, f32[512,512]{1,0:T(8,128)}) custom-call(s32[2]{0:T(128)} %iota.377.pick, s32[2]{0:T(128)} %get-tuple-element.75.coef, s32[4]{0:T(128)} %reshape.79.corner, s32[2]{0:T(128)} %get-tuple-element.74.fill, f32[2,2,256,256]{3,2,1,0:T(8,128)} %collective-permute-done.2.exp_ref.var_ref, ...), custom_call_target="tpu_custom_call" | custom-call | flops 5368709120 | bytes 5242880 | tf_op jit(solution)/shard_map/pallas_call | solution.py:224
  221.8 15.3 %collective-permute-done.9 = f32[512,512]{1,0:T(8,128)} collective-permute-done((f32[512,512]{1,0:T(8,128)}, f32[512,512]{1,0:T(8,128)}, u32[]{:S(2)}, u32[]{:S(2)}) %collective-permute-start.9) | collective-permute-done | bytes 1048608 | tf_op jit(solution)/shard_map/ppermute | solution.py:325
  237.1 2.3 add_divide_fusion.rows_ref
  239.6 3.7 %collective-permute-start.11 = (f32[512,20]{1,0:T(8,128)S(1)}, f32[512,20]{1,0:T(8,128)S(1)}, u32[]{:S(2)}, u32[]{:S(2)}) collective-permute-start(f32[512,20]{1,0:T(8,128)S(1)} %get-tuple-element.82), channel_id=1, source_target_pairs={{0,1},{1,2},{2,3},{4,5},{5,6},{6,7},{8,9},{9,10},{10,11},{12,13},{... | collective-permute-start | bytes 122888 | tf_op jit(solution)/shard_map/ppermute | solution.py:325
  243.3 1.9 collective-permute-start.12
  246.6 4.4 %collective-permute-done.12 = f32[512,20]{1,0:T(8,128)S(1)} collective-permute-done((f32[512,20]{1,0:T(8,128)S(1)}, f32[512,20]{1,0:T(8,128)S(1)}, u32[]{:S(2)}, u32[]{:S(2)}) %collective-permute-start.12) | collective-permute-done | bytes 40992 | tf_op jit(solution)/shard_map/ppermute | solution.py:325
  251.1 1.5 collective-permute-start.14
  253.5 4.0 %shard_map.145.filtered_ref = f32[512,512]{1,0:T(8,128)} custom-call(f32[512,512]{1,0:T(8,128)} %copy-done.1, f32[512,40]{1,0:T(8,128)} %pad_maximum_fusion.edge_ref, f32[512,512]{1,0:T(8,128)} %slice.546.middle_ref, f32[40,512]{1,0:T(8,128)} %pad_maximum_fusion.2.edges_ref), custom_call_target="tpu_custom_call" | custom-call | flops 805306368 | bytes 2260992 | tf_op jit(solution)/shard_map/pallas_call | solution.py:298
  259.7 4.7 %shard_map.146 = f32[512,512]{1,0:T(8,128)} custom-call(f32[512,512]{1,0:T(8,128)} %shard_map.145.filtered_ref, f32[40,512]{1,0:T(8,128)} %fusion.86.near_ref, f32[40,40]{1,0:T(8,128)} %pad_maximum_fusion.5.corner_ref, f32[512,512]{1,0:T(8,128)} %slice.546.middle_ref, f32[40,512]{1,0:T(8,128)} %pad_maximum_fusion.2.edges_ref, f32[512,512]{1,0:T(8,128)} %slice.557.across_ref, ...), custom_call_target="tpu_custom_call" | custom-call | flops 805306368 | bytes 3397888 | tf_op jit(solution)/shard_map/pallas_call | solution.py:298
  (118 shorter events, 34.7 us)
Async XLA Ops:
  0.6 75.9 %copy-start = (f32[64,45]{0,1:T(8,128)S(1)}, f32[64,45]{0,1:T(8,128)}, u32[]{:S(2)}) copy-start(f32[64,45]{0,1:T(8,128)} %param.14) | copy-start | bytes 34564
  3.4 3.1 %copy-start.9 = (s32[1,16,2]{1,2,0:T(2,128)S(1)}, s32[1,16,2]{1,2,0:T(2,128)}, u32[]{:S(2)}) copy-start(s32[1,16,2]{1,2,0:T(2,128)} %param.16) | copy-start | bytes 388
  3.4 3.1 %copy-start.10 = (s32[1,16]{1,0:T(1,128)S(1)}, s32[1,16]{1,0:T(1,128)}, u32[]{:S(2)}) copy-start(s32[1,16]{1,0:T(1,128)} %param.15) | copy-start | bytes 196
  6.3 136.8 %collective-permute-start.8 = (f32[2,2,256,256]{3,2,1,0:T(8,128)}, f32[2,2,256,256]{3,2,1,0:T(8,128)S(1)}, u32[]{:S(2)}, u32[]{:S(2)}) collective-permute-start(f32[2,2,256,256]{3,2,1,0:T(8,128)} %shard_map.138), channel_id=1, source_target_pairs={{0,1},{1,0},{2,3},{3,2},{4,5},{5,4},{6,7},{7,6},{8,9},{9,8},{10,11... | collective-permute-start | bytes 3145736 | tf_op jit(solution)/shard_map/ppermute | solution.py:362
  7.0 106.5 %collective-permute-start.6 = (s32[2,2,4]{2,1,0:T(2,128)S(1)}, s32[2,2,4]{2,1,0:T(2,128)S(1)}, u32[]{:S(2)}, u32[]{:S(2)}) collective-permute-start(s32[2,2,4]{2,1,0:T(2,128)S(1)} %bitcast.140), channel_id=1, source_target_pairs={{0,1},{1,0},{2,3},{3,2},{4,5},{5,4},{6,7},{7,6},{8,9},{9,8},{10,11... | collective-permute-start | bytes 200 | tf_op jit(solution)/shard_map/ppermute | solution.py:362
  10.2 143.3 %collective-permute-start.7 = (f32[2,2,256,256]{3,2,1,0:T(8,128)}, f32[2,2,256,256]{3,2,1,0:T(8,128)}, u32[]{:S(2)}, u32[]{:S(2)}) collective-permute-start(f32[2,2,256,256]{3,2,1,0:T(8,128)} %shard_map.135), channel_id=1, source_target_pairs={{0,1},{1,0},{2,3},{3,2},{4,5},{5,4},{6,7},{7,6},{8,9},{9,8},{10,11... | collective-permute-start | bytes 3145736 | tf_op jit(solution)/shard_map/ppermute | solution.py:362
  10.3 6.9 %copy-start.5 = (f32[41]{0:T(128)S(1)}, f32[41]{0:T(128)}, u32[]{:S(2)}) copy-start(f32[41]{0:T(128)} %param.19) | copy-start | bytes 496
  13.2 150.5 %collective-permute-start.4 = (f32[2,2,256,256]{3,2,1,0:T(8,128)}, f32[2,2,256,256]{3,2,1,0:T(8,128)}, u32[]{:S(2)}, u32[]{:S(2)}) collective-permute-start(f32[2,2,256,256]{3,2,1,0:T(8,128)} %shard_map.134), channel_id=1, source_target_pairs={{0,2},{1,3},{2,0},{3,1},{4,6},{5,7},{6,4},{7,5},{8,10},{9,11},{10,... | collective-permute-start | bytes 3145736 | tf_op jit(solution)/shard_map/ppermute | solution.py:362
  15.9 101.1 %collective-permute-start.3 = (s32[2,2,4]{2,1,0:T(2,128)S(1)}, s32[2,2,4]{2,1,0:T(2,128)S(1)}, u32[]{:S(2)}, u32[]{:S(2)}) collective-permute-start(s32[2,2,4]{2,1,0:T(2,128)S(1)} %bitcast.139), channel_id=1, source_target_pairs={{0,2},{1,3},{2,0},{3,1},{4,6},{5,7},{6,4},{7,5},{8,10},{9,11},{10,... | collective-permute-start | bytes 200 | tf_op jit(solution)/shard_map/ppermute | solution.py:362
  45.2 1.2 copy-start.6
  74.6 1.9 copy-start.7
  74.6 1.9 copy-start.8
  103.6 9.9 %copy-start.4 = (f32[2,2,256,256]{3,2,1,0:T(8,128)S(1)}, f32[2,2,256,256]{3,2,1,0:T(8,128)}, u32[]{:S(2)}) copy-start(f32[2,2,256,256]{3,2,1,0:T(8,128)} %shard_map.132) | copy-start | bytes 3145732
  113.5 50.2 %collective-permute-start.1 = (f32[2,2,256,256]{3,2,1,0:T(8,128)S(1)}, f32[2,2,256,256]{3,2,1,0:T(8,128)}, u32[]{:S(2)}, u32[]{:S(2)}) collective-permute-start(f32[2,2,256,256]{3,2,1,0:T(8,128)S(1)} %copy-done.4), channel_id=1, source_target_pairs={{0,3},{1,2},{2,1},{3,0},{4,7},{5,6},{6,5},{7,4},{8,11},{9,10},{10,... | collective-permute-start | bytes 3145736 | tf_op jit(solution)/shard_map/ppermute | solution.py:362
  117.0 21.8 %collective-permute-start = (s32[2,2,4]{2,1,0:T(2,128)S(1)}, s32[2,2,4]{2,1,0:T(2,128)S(1)}, u32[]{:S(2)}, u32[]{:S(2)}) collective-permute-start(s32[2,2,4]{2,1,0:T(2,128)S(1)} %bitcast.141), channel_id=1, source_target_pairs={{0,3},{1,2},{2,1},{3,0},{4,7},{5,6},{6,5},{7,4},{8,11},{9,10},{10,... | collective-permute-start | bytes 200 | tf_op jit(solution)/shard_map/ppermute | solution.py:362
  143.1 1.0 copy-start.11
  154.1 9.6 %copy-start.3 = (f32[2,2,256,256]{3,2,1,0:T(8,128)S(1)}, f32[2,2,256,256]{3,2,1,0:T(8,128)}, u32[]{:S(2)}) copy-start(f32[2,2,256,256]{3,2,1,0:T(8,128)} %shard_map.133) | copy-start | bytes 3145732
  154.1 11.5 %copy-start.2 = (f32[2,2,256,256]{3,2,1,0:T(8,128)S(1)}, f32[2,2,256,256]{3,2,1,0:T(8,128)}, u32[]{:S(2)}) copy-start(f32[2,2,256,256]{3,2,1,0:T(8,128)} %shard_map.131) | copy-start | bytes 3145732
  163.7 27.6 %collective-permute-start.5 = (f32[2,2,256,256]{3,2,1,0:T(8,128)S(1)}, f32[2,2,256,256]{3,2,1,0:T(8,128)}, u32[]{:S(2)}, u32[]{:S(2)}) collective-permute-start(f32[2,2,256,256]{3,2,1,0:T(8,128)S(1)} %copy-done.3), channel_id=1, source_target_pairs={{0,2},{1,3},{2,0},{3,1},{4,6},{5,7},{6,4},{7,5},{8,10},{9,11},{10,... | collective-permute-start | bytes 3145736 | tf_op jit(solution)/shard_map/ppermute | solution.py:362
  165.6 46.2 %collective-permute-start.2 = (f32[2,2,256,256]{3,2,1,0:T(8,128)S(1)}, f32[2,2,256,256]{3,2,1,0:T(8,128)}, u32[]{:S(2)}, u32[]{:S(2)}) collective-permute-start(f32[2,2,256,256]{3,2,1,0:T(8,128)S(1)} %copy-done.2), channel_id=1, source_target_pairs={{0,3},{1,2},{2,1},{3,0},{4,7},{5,6},{6,5},{7,4},{8,11},{9,10},{10,... | collective-permute-start | bytes 3145736 | tf_op jit(solution)/shard_map/ppermute | solution.py:362
  186.2 35.6 %collective-permute-start.10 = (f32[512,512]{1,0:T(8,128)}, f32[512,512]{1,0:T(8,128)S(1)}, u32[]{:S(2)}, u32[]{:S(2)}) collective-permute-start(f32[512,512]{1,0:T(8,128)} %get-tuple-element.49), channel_id=1, source_target_pairs={{0,4},{1,5},{2,6},{3,7},{4,8},{5,9},{6,10},{7,11},{8,12},{9,13},{1... | collective-permute-start | bytes 3145736 | tf_op jit(solution)/shard_map/ppermute | solution.py:325
  187.9 49.3 %collective-permute-start.9 = (f32[512,512]{1,0:T(8,128)}, f32[512,512]{1,0:T(8,128)}, u32[]{:S(2)}, u32[]{:S(2)}) collective-permute-start(f32[512,512]{1,0:T(8,128)} %get-tuple-element.47), channel_id=1, source_target_pairs={{0,4},{1,5},{2,6},{3,7},{4,8},{5,9},{6,10},{7,11},{8,12},{9,13},{1... | collective-permute-start | bytes 3145736 | tf_op jit(solution)/shard_map/ppermute | solution.py:325
  239.5 14.0 %copy-start.1 = (f32[512,512]{1,0:T(8,128)}, f32[512,512]{1,0:T(8,128)S(1)}, u32[]{:S(2)}) copy-start(f32[512,512]{1,0:T(8,128)S(1)} %add_divide_fusion.rows_ref) | copy-start | bytes 3145732
  239.6 7.0 %collective-permute-start.11 = (f32[512,20]{1,0:T(8,128)S(1)}, f32[512,20]{1,0:T(8,128)S(1)}, u32[]{:S(2)}, u32[]{:S(2)}) collective-permute-start(f32[512,20]{1,0:T(8,128)S(1)} %get-tuple-element.82), channel_id=1, source_target_pairs={{0,1},{1,2},{2,3},{4,5},{5,6},{6,7},{8,9},{9,10},{10,11},{12,13},{... | collective-permute-start | bytes 122888 | tf_op jit(solution)/shard_map/ppermute | solution.py:325
  243.3 7.7 %collective-permute-start.12 = (f32[512,20]{1,0:T(8,128)S(1)}, f32[512,20]{1,0:T(8,128)S(1)}, u32[]{:S(2)}, u32[]{:S(2)}) collective-permute-start(f32[512,20]{1,0:T(8,128)S(1)} %get-tuple-element.83), channel_id=1, source_target_pairs={{1,0},{2,1},{3,2},{5,4},{6,5},{7,6},{9,8},{10,9},{11,10},{13,12},{... | collective-permute-start | bytes 122888 | tf_op jit(solution)/shard_map/ppermute | solution.py:325
  251.1 6.4 %collective-permute-start.14 = (f32[20,552]{1,0:T(8,128)S(1)}, f32[20,552]{1,0:T(8,128)S(1)}, u32[]{:S(2)}, u32[]{:S(2)}) collective-permute-start(f32[20,552]{1,0:T(8,128)S(1)} %pad_maximum_fusion.4), channel_id=1, source_target_pairs={{0,28},{1,29},{2,30},{3,31},{4,0},{5,1},{6,2},{7,3},{8,4},{9,5},{1... | collective-permute-start | bytes 132488 | tf_op jit(solution)/shard_map/ppermute | solution.py:325
  252.6 5.8 %collective-permute-start.13 = (f32[20,552]{1,0:T(8,128)S(1)}, f32[20,552]{1,0:T(8,128)S(1)}, u32[]{:S(2)}, u32[]{:S(2)}) collective-permute-start(f32[20,552]{1,0:T(8,128)S(1)} %pad_maximum_fusion.3), channel_id=1, source_target_pairs={{0,4},{1,5},{2,6},{3,7},{4,8},{5,9},{6,10},{7,11},{8,12},{9,13},{1... | collective-permute-start | bytes 132488 | tf_op jit(solution)/shard_map/ppermute | solution.py:325
where the time goes:
time: 266 us; the launch traced here: 264 us
  Pallas kernels  102 us (38%)
  other arithmetic  60.1 us (23%)
  waiting for transfers between devices  53.5 us (20%)
  local copies, waits for them, and re-layouts  27.8 us (10%)
  starting transfers between devices  17.4 us (7%)
  matrix products  2.9 us (1%)
    pallas_call x8, Pallas kernels, place_tiles(): pl.pallas_call(functools.partial(place_kernel, patch), grid_spec=grid_spe...  76.4 us
    select_n x2, other arithmetic, band(): out = jnp.where(lag == tap, taps[tap], out)  52 us
    ppermute x9, waiting for transfers between devices, swapped(): return lax.ppermute(value, 'src', [(i, i ^ partner) for i in range(owners)])  31.5 us
    ppermute x6, waiting for transfers between devices, shifted(): return lax.ppermute(value, ('sky', 'src'), pairs)  22 us
    pallas_call x6, Pallas kernels, gather_tiles(): pl.pallas_call(gather_kernel, grid_spec=pltpu.PrefetchScalarGridSpec(num_...  16.6 us
    ppermute x6, starting transfers between devices, shifted(): return lax.ppermute(value, ('sky', 'src'), pairs)  9.92 us
    pallas_call x2, Pallas kernels, filter_call(): pl.pallas_call(kernel, out_shape=jax.ShapeDtypeStruct(operands[0].shape,...  8.72 us
    ppermute x9, starting transfers between devices, swapped(): return lax.ppermute(value, 'src', [(i, i ^ partner) for i in range(owners)])  7.47 us
  transfers between devices with their start and end apart: 15, of which 6 were waited for; matrix products, arithmetic and copies ran while one was open for 32% of the time, Pallas kernels for 36%

commit v1 on v0

--- a/solution.py
+++ b/solution.py
@@ -261,14 +261,23 @@
     )(pick, tiles, variance)
 
 
+def band_kernel(taps_ref, out_ref):
+    spread = jnp.broadcast_to(taps_ref[...], out_ref.shape)
+    out_ref[...] = pltpu.roll(spread, 0, 1, stride=1, stride_axis=0)
+
+
 def band(taps, outputs):
     size = taps.shape[0]
-    shape = (outputs + size - 1, outputs)
-    lag = lax.broadcasted_iota(jnp.int32, shape, 0) - lax.broadcasted_iota(jnp.int32, shape, 1)
-    out = jnp.zeros(shape, jnp.float32)
-    for tap in range(size):
-        out = jnp.where(lag == tap, taps[tap], out)
-    return out
+    width = outputs + LANES
+    row = jnp.concatenate([taps, jnp.zeros((width - size,), jnp.float32)])[None]
+    wide = pl.pallas_call(
+        band_kernel,
+        out_shape=jax.ShapeDtypeStruct((outputs, width), jnp.float32),
+        in_specs=[pl.BlockSpec(memory_space=pltpu.VMEM)],
+        out_specs=pl.BlockSpec(memory_space=pltpu.VMEM),
+        compiler_params=pltpu.CompilerParams(vmem_limit_bytes=VMEM),
+    )(row)
+    return wide[:, : outputs + size - 1]
 
 
 def inner_and_rims(matrix, rim, axis):
@@ -411,8 +420,8 @@
     coadd = (here[0] + moved[0]) / (here[1] + moved[1] + 1.0)
 
     rim = detect_ra.shape[0] // 2
-    along_dec = band(detect_dec, patch)
-    along_ra = band(detect_ra, patch).T
+    along_dec = band(detect_dec, patch).T
+    along_ra = band(detect_ra, patch)
     left = shifted(coadd[:, patch - rim :], 0, 1)
     right = shifted(coadd[:, :rim], 0, -1)
 

time: 266 us -> 218 us (0.82)
  other arithmetic: 60.1 us -> 8.15 us
  Pallas kernels: 102 us -> 106 us
    select_n x2 -> x0, other arithmetic: 52 us -> none  [band(): out = jnp.where(lag == tap, taps[tap], out)]
    slice x6 -> x0, local copies, waits for them, and re-layouts: 4.04 us -> none  [band(): out = jnp.where(lag == tap, taps[tap], out)]
    pallas_call x0 -> x2, Pallas kernels: none -> 3.85 us  [band(): pl.pallas_call(band_kernel, out_shape=jax.ShapeDtypeStruct((outputs, widt...]
  transfers between devices with their start and end apart: 15 -> 15, of which waited for: 6 -> 6; matrix products, arithmetic and copies ran while one was open for 32% -> 15% of each run, Pallas kernels for 36% -> 45%
where the time goes in v1:
time: 218 us; the launch traced here: 217 us
  Pallas kernels  106 us (49%)
  waiting for transfers between devices  53.3 us (24%)
  local copies, waits for them, and re-layouts  28.5 us (13%)
  starting transfers between devices  17.6 us (8%)
  other arithmetic  8.15 us (4%)
  matrix products  2.91 us (1%)
    pallas_call x8, Pallas kernels, place_tiles(): pl.pallas_call(functools.partial(place_kernel, patch), grid_spec=grid_spe...  76.8 us
    ppermute x9, waiting for transfers between devices, swapped(): return lax.ppermute(value, 'src', [(i, i ^ partner) for i in range(owners)])  31.6 us
    ppermute x6, waiting for transfers between devices, shifted(): return lax.ppermute(value, ('sky', 'src'), pairs)  21.7 us
    pallas_call x6, Pallas kernels, gather_tiles(): pl.pallas_call(gather_kernel, grid_spec=pltpu.PrefetchScalarGridSpec(num_...  16.7 us
    ppermute x6, starting transfers between devices, shifted(): return lax.ppermute(value, ('sky', 'src'), pairs)  10 us
    pallas_call x2, Pallas kernels, filter_call(): pl.pallas_call(kernel, out_shape=jax.ShapeDtypeStruct(operands[0].shape,...  8.72 us
    ppermute x9, starting transfers between devices, swapped(): return lax.ppermute(value, 'src', [(i, i ^ partner) for i in range(owners)])  7.63 us
    slice x15, local copies, waits for them, and re-layouts, add(): note = (note[:, 0], note[:, 1:3], note[:, 3])  5.93 us
  transfers between devices with their start and end apart: 15, of which 6 were waited for; matrix products, arithmetic and copies ran while one was open for 15% of the time, Pallas kernels for 45%

profile of v1, /device:TPU:1, one launch (start us, length us, event | category | flops | bytes accessed | tf_op | source)
XLA Modules:
  0.0 217.4 jit_solution(3680728442917165358)
XLA Ops:
  3.4 2.8 %shard_map.138 = f32[2,2,256,256]{3,2,1,0:T(8,128)} custom-call(s32[2]{0:T(128)} %get-tuple-element.103.pick, f32[16,256,256]{2,1,0:T(8,128)} %bitcast.35, f32[16,256,256]{2,1,0:T(8,128)} %bitcast.41), custom_call_target="tpu_custom_call" | custom-call | bytes 2097152 | tf_op jit(solution)/shard_map/pallas_call | solution.py:248
  7.5 2.8 %shard_map.135 = f32[2,2,256,256]{3,2,1,0:T(8,128)} custom-call(s32[2]{0:T(128)} %get-tuple-element.67.pick, f32[16,256,256]{2,1,0:T(8,128)} %bitcast.36, f32[16,256,256]{2,1,0:T(8,128)} %bitcast.42), custom_call_target="tpu_custom_call" | custom-call | bytes 2097152 | tf_op jit(solution)/shard_map/pallas_call | solution.py:248
  10.3 2.9 %shard_map.134 = f32[2,2,256,256]{3,2,1,0:T(8,128)} custom-call(s32[2]{0:T(128)} %get-tuple-element.68.pick, f32[16,256,256]{2,1,0:T(8,128)} %bitcast.37, f32[16,256,256]{2,1,0:T(8,128)} %bitcast.43), custom_call_target="tpu_custom_call" | custom-call | bytes 2097152 | tf_op jit(solution)/shard_map/pallas_call | solution.py:248
  13.2 2.7 %collective-permute-start.4 = (f32[2,2,256,256]{3,2,1,0:T(8,128)}, f32[2,2,256,256]{3,2,1,0:T(8,128)}, u32[]{:S(2)}, u32[]{:S(2)}) collective-permute-start(f32[2,2,256,256]{3,2,1,0:T(8,128)} %shard_map.134), channel_id=1, source_target_pairs={{0,2},{1,3},{2,0},{3,1},{4,6},{5,7},{6,4},{7,5},{8,10},{9,11},{10,... | collective-permute-start | bytes 3145736 | tf_op jit(solution)/shard_map/ppermute | solution.py:371
  17.9 1.9 shard_map.145
  19.8 1.7 copy.60
  23.2 1.9 shard_map.147
  26.3 2.6 %slice.238.across_ref = f32[512,512]{1,0:T(8,128)} slice(f32[512,640]{1,0:T(8,128)} %shard_map.147), slice={[0:512], [20:532]} | slice | bytes 2097152 | tf_op jit(solution)/shard_map/slice | solution.py:286
  29.5 2.9 %fusion = f32[21,512,64]{1,2,0:T(8,128)S(1)} fusion(f32[45,512]{1,0:T(8,128)S(1)} %copy-done.5, f32[45,21]{0,1:T(8,128)S(1)} %copy-done.6, f32[64,45]{0,1:T(8,128)S(1)} %copy-done), kind=kOutput, calls=%fused_computation.1 | convolution fusion | flops 372072960 | bytes 2859972 | tf_op jit(solution)/shard_map/ck,ksl->csl/dot_general | solution.py:365
  32.5 3.3 %copy.62 = f32[21,512,64]{1,0,2:T(8,128)} copy(f32[21,512,64]{1,2,0:T(8,128)S(1)} %fusion) | data formatting | bytes 5505024 | tf_op jit(solution)/shard_map/ck,ksl->csl/dot_general | solution.py:365
  36.4 2.7 %shard_map.133 = f32[2,2,256,256]{3,2,1,0:T(8,128)} custom-call(s32[2]{0:T(128)} %get-tuple-element.102.pick, f32[16,256,256]{2,1,0:T(8,128)} %bitcast.38, f32[16,256,256]{2,1,0:T(8,128)} %bitcast.44), custom_call_target="tpu_custom_call" | custom-call | bytes 2097152 | tf_op jit(solution)/shard_map/pallas_call | solution.py:248
  39.1 2.7 %shard_map.132 = f32[2,2,256,256]{3,2,1,0:T(8,128)} custom-call(s32[2]{0:T(128)} %get-tuple-element.69.pick, f32[16,256,256]{2,1,0:T(8,128)} %bitcast.39, f32[16,256,256]{2,1,0:T(8,128)} %bitcast.45), custom_call_target="tpu_custom_call" | custom-call | bytes 2097152 | tf_op jit(solution)/shard_map/pallas_call | solution.py:248
  41.8 2.7 %shard_map.131 = f32[2,2,256,256]{3,2,1,0:T(8,128)} custom-call(s32[2]{0:T(128)} %get-tuple-element.101.pick, f32[16,256,256]{2,1,0:T(8,128)} %bitcast.40, f32[16,256,256]{2,1,0:T(8,128)} %bitcast.46), custom_call_target="tpu_custom_call" | custom-call | bytes 2097152 | tf_op jit(solution)/shard_map/pallas_call | solution.py:248
  47.2 9.6 %shard_map.139 = (f32[512,512]{1,0:T(8,128)}, f32[512,512]{1,0:T(8,128)}) custom-call(s32[2]{0:T(128)} %get-tuple-element.104.pick, s32[2]{0:T(128)} %get-tuple-element.57.coef, s32[4]{0:T(128)} %reshape.84.corner, s32[2]{0:T(128)} %get-tuple-element.56.fill, f32[1,16,256,256]{3,2,1,0:T(8,128)} %exp_ref.3, f32[1,16,256,256]{3,2,1,0:T(8,128)} %var_ref.3, ...), custom_call_target="tpu_custom_call" | custom-call | flops 5368709120 | bytes 5242880 | tf_op jit(solution)/shard_map/pallas_call | solution.py:224
  56.9 10.0 %shard_map.136 = (f32[512,512]{1,0:T(8,128)}, f32[512,512]{1,0:T(8,128)}) custom-call(s32[2]{0:T(128)} %get-tuple-element.66.pick, s32[2]{0:T(128)} %get-tuple-element.105.coef, s32[4]{0:T(128)} %reshape.82.corner, s32[2]{0:T(128)} %get-tuple-element.106.fill, f32[1,16,256,256]{3,2,1,0:T(8,128)} %exp_ref.3, f32[1,16,256,256]{3,2,1,0:T(8,128)} %var_ref.3, ...), custom_call_target="tpu_custom_call" | custom-call | flops 5368709120 | bytes 5242880 | tf_op jit(solution)/shard_map/pallas_call | solution.py:224
  67.0 2.0 collective-permute-start.1
  71.3 21.0 %collective-permute-done = s32[2,2,4]{2,1,0:T(2,128)S(1)} collective-permute-done((s32[2,2,4]{2,1,0:T(2,128)S(1)}, s32[2,2,4]{2,1,0:T(2,128)S(1)}, u32[]{:S(2)}, u32[]{:S(2)}) %collective-permute-start) | collective-permute-done | bytes 96 | tf_op jit(solution)/shard_map/ppermute | solution.py:371
  97.1 9.5 %shard_map.140 = (f32[512,512]{1,0:T(8,128)}, f32[512,512]{1,0:T(8,128)}) custom-call(s32[2]{0:T(128)} %iota.42.pick, s32[2]{0:T(128)} %get-tuple-element.63.coef, s32[4]{0:T(128)} %reshape.83.corner, s32[2]{0:T(128)} %get-tuple-element.62.fill, f32[2,2,256,256]{3,2,1,0:T(8,128)} %collective-permute-done.8.exp_ref.var_ref, ...), custom_call_target="tpu_custom_call" | custom-call | flops 5368709120 | bytes 5242880 | tf_op jit(solution)/shard_map/pallas_call | solution.py:224
  107.1 9.6 %shard_map.137 = (f32[512,512]{1,0:T(8,128)}, f32[512,512]{1,0:T(8,128)}) custom-call(s32[2]{0:T(128)} %iota.41.pick, s32[2]{0:T(128)} %get-tuple-element.71.coef, s32[4]{0:T(128)} %reshape.81.corner, s32[2]{0:T(128)} %get-tuple-element.70.fill, f32[2,2,256,256]{3,2,1,0:T(8,128)} %collective-permute-done.7.exp_ref.var_ref, ...), custom_call_target="tpu_custom_call" | custom-call | flops 5368709120 | bytes 5242880 | tf_op jit(solution)/shard_map/pallas_call | solution.py:224
  116.7 2.0 collective-permute-start.5
  119.6 9.5 %shard_map.143 = (f32[512,512]{1,0:T(8,128)}, f32[512,512]{1,0:T(8,128)}) custom-call(s32[2]{0:T(128)} %iota.44.pick, s32[2]{0:T(128)} %get-tuple-element.53.coef, s32[4]{0:T(128)} %reshape.86.corner, s32[2]{0:T(128)} %get-tuple-element.52.fill, f32[2,2,256,256]{3,2,1,0:T(8,128)} %collective-permute-done.4.exp_ref.var_ref, ...), custom_call_target="tpu_custom_call" | custom-call | flops 5368709120 | bytes 5242880 | tf_op jit(solution)/shard_map/pallas_call | solution.py:224
  129.6 9.7 %shard_map.144 = (f32[512,512]{1,0:T(8,128)}, f32[512,512]{1,0:T(8,128)}) custom-call(s32[2]{0:T(128)} %iota.43.pick, s32[2]{0:T(128)} %get-tuple-element.55.coef, s32[4]{0:T(128)} %reshape.85.corner, s32[2]{0:T(128)} %get-tuple-element.54.fill, f32[2,2,256,256]{3,2,1,0:T(8,128)} %collective-permute-done.1.exp_ref.var_ref, ...), custom_call_target="tpu_custom_call" | custom-call | flops 5368709120 | bytes 5242880 | tf_op jit(solution)/shard_map/pallas_call | solution.py:224
  144.8 9.5 %shard_map.141 = (f32[512,512]{1,0:T(8,128)}, f32[512,512]{1,0:T(8,128)}) custom-call(s32[2]{0:T(128)} %iota.40.pick, s32[2]{0:T(128)} %get-tuple-element.73.coef, s32[4]{0:T(128)} %reshape.80.corner, s32[2]{0:T(128)} %get-tuple-element.72.fill, f32[2,2,256,256]{3,2,1,0:T(8,128)} %collective-permute-done.5.exp_ref.var_ref, ...), custom_call_target="tpu_custom_call" | custom-call | flops 5368709120 | bytes 5242880 | tf_op jit(solution)/shard_map/pallas_call | solution.py:224
  154.3 10.6 %collective-permute-done.2.exp_ref.var_ref = f32[2,2,256,256]{3,2,1,0:T(8,128)} collective-permute-done((f32[2,2,256,256]{3,2,1,0:T(8,128)S(1)}, f32[2,2,256,256]{3,2,1,0:T(8,128)}, u32[]{:S(2)}, u32[]{:S(2)}) %collective-permute-start.2) | collective-permute-done | bytes 1048608 | tf_op jit(solution)/shard_map/ppermute | solution.py:371
  165.4 9.5 %shard_map.142 = (f32[512,512]{1,0:T(8,128)}, f32[512,512]{1,0:T(8,128)}) custom-call(s32[2]{0:T(128)} %iota.37.pick, s32[2]{0:T(128)} %get-tuple-element.75.coef, s32[4]{0:T(128)} %reshape.79.corner, s32[2]{0:T(128)} %get-tuple-element.74.fill, f32[2,2,256,256]{3,2,1,0:T(8,128)} %collective-permute-done.2.exp_ref.var_ref, ...), custom_call_target="tpu_custom_call" | custom-call | flops 5368709120 | bytes 5242880 | tf_op jit(solution)/shard_map/pallas_call | solution.py:224
  175.0 15.0 %collective-permute-done.9 = f32[512,512]{1,0:T(8,128)} collective-permute-done((f32[512,512]{1,0:T(8,128)}, f32[512,512]{1,0:T(8,128)}, u32[]{:S(2)}, u32[]{:S(2)}) %collective-permute-start.9) | collective-permute-done | bytes 1048608 | tf_op jit(solution)/shard_map/ppermute | solution.py:334
  190.0 2.3 %add_divide_fusion.rows_ref = f32[512,512]{1,0:T(8,128)S(1)} fusion(f32[512,512]{1,0:T(8,128)} %get-tuple-element.48, f32[512,512]{1,0:T(8,128)S(1)} %collective-permute-done.10, f32[512,512]{1,0:T(8,128)} %get-tuple-element.40, f32[512,512]{1,0:T(8,128)} %collective-permute-done.9), kind=kLoop, calls=%fused_computation.3 | loop fusion | flops 1048576 | bytes 5242880 | tf_op jit(solution)/shard_map/div | solution.py:420
  192.5 3.8 %collective-permute-start.11 = (f32[512,20]{1,0:T(8,128)S(1)}, f32[512,20]{1,0:T(8,128)S(1)}, u32[]{:S(2)}, u32[]{:S(2)}) collective-permute-start(f32[512,20]{1,0:T(8,128)S(1)} %get-tuple-element.82), channel_id=1, source_target_pairs={{0,1},{1,2},{2,3},{4,5},{5,6},{6,7},{8,9},{9,10},{10,11},{12,13},{... | collective-permute-start | bytes 122888 | tf_op jit(solution)/shard_map/ppermute | solution.py:334
  196.4 1.9 collective-permute-start.12
  199.6 4.4 %collective-permute-done.12 = f32[512,20]{1,0:T(8,128)S(1)} collective-permute-done((f32[512,20]{1,0:T(8,128)S(1)}, f32[512,20]{1,0:T(8,128)S(1)}, u32[]{:S(2)}, u32[]{:S(2)}) %collective-permute-start.12) | collective-permute-done | bytes 40992 | tf_op jit(solution)/shard_map/ppermute | solution.py:334
  206.5 4.0 %shard_map.146.filtered_ref = f32[512,512]{1,0:T(8,128)} custom-call(f32[512,512]{1,0:T(8,128)} %copy-done.1, f32[512,40]{1,0:T(8,128)} %pad_maximum_fusion.edge_ref, f32[512,512]{1,0:T(8,128)} %slice.227.middle_ref, f32[40,512]{1,0:T(8,128)} %pad_maximum_fusion.2.edges_ref), custom_call_target="tpu_custom_call" | custom-call | flops 805306368 | bytes 2260992 | tf_op jit(solution)/shard_map/pallas_call | solution.py:307
  212.7 4.7 %shard_map.148 = f32[512,512]{1,0:T(8,128)} custom-call(f32[512,512]{1,0:T(8,128)} %shard_map.146.filtered_ref, f32[40,512]{1,0:T(8,128)} %fusion.4.near_ref, f32[40,40]{1,0:T(8,128)} %pad_maximum_fusion.5.corner_ref, f32[512,512]{1,0:T(8,128)} %slice.227.middle_ref, f32[40,512]{1,0:T(8,128)} %pad_maximum_fusion.2.edges_ref, f32[512,512]{1,0:T(8,128)} %slice.238.across_ref, ...), custom_call_target="tpu_custom_call" | custom-call | flops 805306368 | bytes 3397888 | tf_op jit(solution)/shard_map/pallas_call | solution.py:307
  (115 shorter events, 34.2 us)
Async XLA Ops:
  0.6 28.9 %copy-start = (f32[64,45]{0,1:T(8,128)S(1)}, f32[64,45]{0,1:T(8,128)}, u32[]{:S(2)}) copy-start(f32[64,45]{0,1:T(8,128)} %param.14) | copy-start | bytes 34564
  3.4 3.1 %copy-start.7 = (s32[1,16,2]{1,2,0:T(2,128)S(1)}, s32[1,16,2]{1,2,0:T(2,128)}, u32[]{:S(2)}) copy-start(s32[1,16,2]{1,2,0:T(2,128)} %param.16) | copy-start | bytes 388
  3.4 3.1 %copy-start.8 = (s32[1,16]{1,0:T(1,128)S(1)}, s32[1,16]{1,0:T(1,128)}, u32[]{:S(2)}) copy-start(s32[1,16]{1,0:T(1,128)} %param.15) | copy-start | bytes 196
  6.3 90.3 %collective-permute-start.8 = (f32[2,2,256,256]{3,2,1,0:T(8,128)}, f32[2,2,256,256]{3,2,1,0:T(8,128)}, u32[]{:S(2)}, u32[]{:S(2)}) collective-permute-start(f32[2,2,256,256]{3,2,1,0:T(8,128)} %shard_map.138), channel_id=1, source_target_pairs={{0,1},{1,0},{2,3},{3,2},{4,5},{5,4},{6,7},{7,6},{8,9},{9,8},{10,11... | collective-permute-start | bytes 3145736 | tf_op jit(solution)/shard_map/ppermute | solution.py:371
  7.0 59.9 %collective-permute-start.6 = (s32[2,2,4]{2,1,0:T(2,128)S(1)}, s32[2,2,4]{2,1,0:T(2,128)S(1)}, u32[]{:S(2)}, u32[]{:S(2)}) collective-permute-start(s32[2,2,4]{2,1,0:T(2,128)S(1)} %bitcast.63), channel_id=1, source_target_pairs={{0,1},{1,0},{2,3},{3,2},{4,5},{5,4},{6,7},{7,6},{8,9},{9,8},{10,11... | collective-permute-start | bytes 200 | tf_op jit(solution)/shard_map/ppermute | solution.py:371
  10.3 96.3 %collective-permute-start.7 = (f32[2,2,256,256]{3,2,1,0:T(8,128)}, f32[2,2,256,256]{3,2,1,0:T(8,128)}, u32[]{:S(2)}, u32[]{:S(2)}) collective-permute-start(f32[2,2,256,256]{3,2,1,0:T(8,128)} %shard_map.135), channel_id=1, source_target_pairs={{0,1},{1,0},{2,3},{3,2},{4,5},{5,4},{6,7},{7,6},{8,9},{9,8},{10,11... | collective-permute-start | bytes 3145736 | tf_op jit(solution)/shard_map/ppermute | solution.py:371
  10.3 6.9 %copy-start.9 = (f32[41]{0:T(128)S(1)}, f32[41]{0:T(128)}, u32[]{:S(2)}) copy-start(f32[41]{0:T(128)} %param.19) | copy-start | bytes 496
  13.2 103.4 %collective-permute-start.4 = (f32[2,2,256,256]{3,2,1,0:T(8,128)}, f32[2,2,256,256]{3,2,1,0:T(8,128)}, u32[]{:S(2)}, u32[]{:S(2)}) collective-permute-start(f32[2,2,256,256]{3,2,1,0:T(8,128)} %shard_map.134), channel_id=1, source_target_pairs={{0,2},{1,3},{2,0},{3,1},{4,6},{5,7},{6,4},{7,5},{8,10},{9,11},{10,... | collective-permute-start | bytes 3145736 | tf_op jit(solution)/shard_map/ppermute | solution.py:371
  16.0 54.5 %collective-permute-start.3 = (s32[2,2,4]{2,1,0:T(2,128)S(1)}, s32[2,2,4]{2,1,0:T(2,128)S(1)}, u32[]{:S(2)}, u32[]{:S(2)}) collective-permute-start(s32[2,2,4]{2,1,0:T(2,128)S(1)} %bitcast.62), channel_id=1, source_target_pairs={{0,2},{1,3},{2,0},{3,1},{4,6},{5,7},{6,4},{7,5},{8,10},{9,11},{10,... | collective-permute-start | bytes 200 | tf_op jit(solution)/shard_map/ppermute | solution.py:371
  19.8 2.8 %copy-start.10 = (f32[41]{0:T(128)S(1)}, f32[41]{0:T(128)}, u32[]{:S(2)}) copy-start(f32[41]{0:T(128)} %param.18) | copy-start | bytes 496
  23.2 6.4 %copy-start.5 = (f32[45,512]{1,0:T(8,128)S(1)}, f32[45,512]{1,0:T(8,128)}, u32[]{:S(2)}) copy-start(f32[45,512]{1,0:T(8,128)} %constant.60.clone) | copy-start | bytes 276484
  23.2 6.4 %copy-start.6 = (f32[45,21]{0,1:T(8,128)S(1)}, f32[45,21]{0,1:T(8,128)}, u32[]{:S(2)}) copy-start(f32[45,21]{0,1:T(8,128)} %constant.59.clone) | copy-start | bytes 11344
  56.9 10.1 %copy-start.4 = (f32[2,2,256,256]{3,2,1,0:T(8,128)S(1)}, f32[2,2,256,256]{3,2,1,0:T(8,128)}, u32[]{:S(2)}) copy-start(f32[2,2,256,256]{3,2,1,0:T(8,128)} %shard_map.132) | copy-start | bytes 3145732
  67.0 49.7 %collective-permute-start.1 = (f32[2,2,256,256]{3,2,1,0:T(8,128)S(1)}, f32[2,2,256,256]{3,2,1,0:T(8,128)}, u32[]{:S(2)}, u32[]{:S(2)}) collective-permute-start(f32[2,2,256,256]{3,2,1,0:T(8,128)S(1)} %copy-done.4), channel_id=1, source_target_pairs={{0,3},{1,2},{2,1},{3,0},{4,7},{5,6},{6,5},{7,4},{8,11},{9,10},{10,... | collective-permute-start | bytes 3145736 | tf_op jit(solution)/shard_map/ppermute | solution.py:371
  70.5 21.8 %collective-permute-start = (s32[2,2,4]{2,1,0:T(2,128)S(1)}, s32[2,2,4]{2,1,0:T(2,128)S(1)}, u32[]{:S(2)}, u32[]{:S(2)}) collective-permute-start(s32[2,2,4]{2,1,0:T(2,128)S(1)} %bitcast.64), channel_id=1, source_target_pairs={{0,3},{1,2},{2,1},{3,0},{4,7},{5,6},{6,5},{7,4},{8,11},{9,10},{10,... | collective-permute-start | bytes 200 | tf_op jit(solution)/shard_map/ppermute | solution.py:371
  107.1 9.6 %copy-start.3 = (f32[2,2,256,256]{3,2,1,0:T(8,128)S(1)}, f32[2,2,256,256]{3,2,1,0:T(8,128)}, u32[]{:S(2)}) copy-start(f32[2,2,256,256]{3,2,1,0:T(8,128)} %shard_map.133) | copy-start | bytes 3145732
  107.1 11.6 %copy-start.2 = (f32[2,2,256,256]{3,2,1,0:T(8,128)S(1)}, f32[2,2,256,256]{3,2,1,0:T(8,128)}, u32[]{:S(2)}) copy-start(f32[2,2,256,256]{3,2,1,0:T(8,128)} %shard_map.131) | copy-start | bytes 3145732
  116.7 27.6 %collective-permute-start.5 = (f32[2,2,256,256]{3,2,1,0:T(8,128)S(1)}, f32[2,2,256,256]{3,2,1,0:T(8,128)}, u32[]{:S(2)}, u32[]{:S(2)}) collective-permute-start(f32[2,2,256,256]{3,2,1,0:T(8,128)S(1)} %copy-done.3), channel_id=1, source_target_pairs={{0,2},{1,3},{2,0},{3,1},{4,6},{5,7},{6,4},{7,5},{8,10},{9,11},{10,... | collective-permute-start | bytes 3145736 | tf_op jit(solution)/shard_map/ppermute | solution.py:371
  118.7 46.2 %collective-permute-start.2 = (f32[2,2,256,256]{3,2,1,0:T(8,128)S(1)}, f32[2,2,256,256]{3,2,1,0:T(8,128)}, u32[]{:S(2)}, u32[]{:S(2)}) collective-permute-start(f32[2,2,256,256]{3,2,1,0:T(8,128)S(1)} %copy-done.2), channel_id=1, source_target_pairs={{0,3},{1,2},{2,1},{3,0},{4,7},{5,6},{6,5},{7,4},{8,11},{9,10},{10,... | collective-permute-start | bytes 3145736 | tf_op jit(solution)/shard_map/ppermute | solution.py:371
  139.3 35.6 %collective-permute-start.10 = (f32[512,512]{1,0:T(8,128)}, f32[512,512]{1,0:T(8,128)S(1)}, u32[]{:S(2)}, u32[]{:S(2)}) collective-permute-start(f32[512,512]{1,0:T(8,128)} %get-tuple-element.49), channel_id=1, source_target_pairs={{0,4},{1,5},{2,6},{3,7},{4,8},{5,9},{6,10},{7,11},{8,12},{9,13},{1... | collective-permute-start | bytes 3145736 | tf_op jit(solution)/shard_map/ppermute | solution.py:334
  140.8 49.1 %collective-permute-start.9 = (f32[512,512]{1,0:T(8,128)}, f32[512,512]{1,0:T(8,128)}, u32[]{:S(2)}, u32[]{:S(2)}) collective-permute-start(f32[512,512]{1,0:T(8,128)} %get-tuple-element.47), channel_id=1, source_target_pairs={{0,4},{1,5},{2,6},{3,7},{4,8},{5,9},{6,10},{7,11},{8,12},{9,13},{1... | collective-permute-start | bytes 3145736 | tf_op jit(solution)/shard_map/ppermute | solution.py:334
  192.3 14.2 %copy-start.1 = (f32[512,512]{1,0:T(8,128)}, f32[512,512]{1,0:T(8,128)S(1)}, u32[]{:S(2)}) copy-start(f32[512,512]{1,0:T(8,128)S(1)} %add_divide_fusion.rows_ref) | copy-start | bytes 3145732
  192.5 7.1 %collective-permute-start.11 = (f32[512,20]{1,0:T(8,128)S(1)}, f32[512,20]{1,0:T(8,128)S(1)}, u32[]{:S(2)}, u32[]{:S(2)}) collective-permute-start(f32[512,20]{1,0:T(8,128)S(1)} %get-tuple-element.82), channel_id=1, source_target_pairs={{0,1},{1,2},{2,3},{4,5},{5,6},{6,7},{8,9},{9,10},{10,11},{12,13},{... | collective-permute-start | bytes 122888 | tf_op jit(solution)/shard_map/ppermute | solution.py:334
  196.4 7.7 %collective-permute-start.12 = (f32[512,20]{1,0:T(8,128)S(1)}, f32[512,20]{1,0:T(8,128)S(1)}, u32[]{:S(2)}, u32[]{:S(2)}) collective-permute-start(f32[512,20]{1,0:T(8,128)S(1)} %get-tuple-element.83), channel_id=1, source_target_pairs={{1,0},{2,1},{3,2},{5,4},{6,5},{7,6},{9,8},{10,9},{11,10},{13,12},{... | collective-permute-start | bytes 122888 | tf_op jit(solution)/shard_map/ppermute | solution.py:334
  204.1 6.4 %collective-permute-start.14 = (f32[20,552]{1,0:T(8,128)S(1)}, f32[20,552]{1,0:T(8,128)S(1)}, u32[]{:S(2)}, u32[]{:S(2)}) collective-permute-start(f32[20,552]{1,0:T(8,128)S(1)} %pad_maximum_fusion.4), channel_id=1, source_target_pairs={{0,28},{1,29},{2,30},{3,31},{4,0},{5,1},{6,2},{7,3},{8,4},{9,5},{1... | collective-permute-start | bytes 132488 | tf_op jit(solution)/shard_map/ppermute | solution.py:334
  205.6 5.8 %collective-permute-start.13 = (f32[20,552]{1,0:T(8,128)S(1)}, f32[20,552]{1,0:T(8,128)S(1)}, u32[]{:S(2)}, u32[]{:S(2)}) collective-permute-start(f32[20,552]{1,0:T(8,128)S(1)} %pad_maximum_fusion.3), channel_id=1, source_target_pairs={{0,4},{1,5},{2,6},{3,7},{4,8},{5,9},{6,10},{7,11},{8,12},{9,13},{1... | collective-permute-start | bytes 132488 | tf_op jit(solution)/shard_map/ppermute | solution.py:334

commit v2 on v1

--- a/solution.py
+++ b/solution.py
@@ -411,7 +411,6 @@
     ahead = add(ahead, 1, 1, arrived[1, 1])
     here = add((zero, zero), 0, 0, None)
     here = add(here, 0, 1, arrived[0, 1])
-    ahead, here = lax.optimization_barrier((ahead, here))
     for partner in far:
         ahead = add(ahead, 1, partner, arrived[1, partner])
     moved = [shifted(value, 1, 0) for value in ahead]

time: 218 us -> 189 us (0.87)
  waiting for transfers between devices: 53.3 us -> 25.1 us
    ppermute x9, waiting for transfers between devices: 31.6 us -> 1.33 us  [swapped(): return lax.ppermute(value, 'src', [(i, i ^ partner) for i in range(owners)])]
  transfers between devices with their start and end apart: 15 -> 15, of which waited for: 6 -> 5; matrix products, arithmetic and copies ran while one was open for 15% -> 18% of each run, Pallas kernels for 45% -> 52%
where the time goes in v2:
time: 189 us; the launch traced here: 188 us
  Pallas kernels  106 us (56%)
  local copies, waits for them, and re-layouts  29 us (15%)
  waiting for transfers between devices  25.1 us (13%)
  starting transfers between devices  16.6 us (9%)
  other arithmetic  8.12 us (4%)
  matrix products  2.9 us (2%)
    pallas_call x8, Pallas kernels, place_tiles(): pl.pallas_call(functools.partial(place_kernel, patch), grid_spec=grid_spe...  76.2 us
    ppermute x6, waiting for transfers between devices, shifted(): return lax.ppermute(value, ('sky', 'src'), pairs)  23.8 us
    pallas_call x6, Pallas kernels, gather_tiles(): pl.pallas_call(gather_kernel, grid_spec=pltpu.PrefetchScalarGridSpec(num_...  16.7 us
    ppermute x6, starting transfers between devices, shifted(): return lax.ppermute(value, ('sky', 'src'), pairs)  9.97 us
    pallas_call x2, Pallas kernels, filter_call(): pl.pallas_call(kernel, out_shape=jax.ShapeDtypeStruct(operands[0].shape,...  8.73 us
    ppermute x9, starting transfers between devices, swapped(): return lax.ppermute(value, 'src', [(i, i ^ partner) for i in range(owners)])  6.61 us
    slice x15, local copies, waits for them, and re-layouts, add(): note = (note[:, 0], note[:, 1:3], note[:, 3])  5.82 us
    reshape x8, local copies, waits for them, and re-layouts, place_tiles(): corner.reshape(-1)  5.14 us
  transfers between devices with their start and end apart: 15, of which 5 were waited for; matrix products, arithmetic and copies ran while one was open for 18% of the time, Pallas kernels for 52%

profile of v2, /device:TPU:1, one launch (start us, length us, event | category | flops | bytes accessed | tf_op | source)
XLA Modules:
  0.0 188.1 jit_solution(14256445418790280853)
XLA Ops:
  3.4 2.9 %shard_map.140 = f32[2,2,256,256]{3,2,1,0:T(8,128)} custom-call(s32[2]{0:T(128)} %get-tuple-element.95.pick, f32[16,256,256]{2,1,0:T(8,128)} %bitcast.35, f32[16,256,256]{2,1,0:T(8,128)} %bitcast.41), custom_call_target="tpu_custom_call" | custom-call | bytes 2097152 | tf_op jit(solution)/shard_map/pallas_call | solution.py:248
  7.5 2.7 %shard_map.134 = f32[2,2,256,256]{3,2,1,0:T(8,128)} custom-call(s32[2]{0:T(128)} %get-tuple-element.94.pick, f32[16,256,256]{2,1,0:T(8,128)} %bitcast.36, f32[16,256,256]{2,1,0:T(8,128)} %bitcast.42), custom_call_target="tpu_custom_call" | custom-call | bytes 2097152 | tf_op jit(solution)/shard_map/pallas_call | solution.py:248
  10.2 2.2 %collective-permute-start.4 = (f32[2,2,256,256]{3,2,1,0:T(8,128)}, f32[2,2,256,256]{3,2,1,0:T(8,128)}, u32[]{:S(2)}, u32[]{:S(2)}) collective-permute-start(f32[2,2,256,256]{3,2,1,0:T(8,128)} %shard_map.134), channel_id=1, source_target_pairs={{0,2},{1,3},{2,0},{3,1},{4,6},{5,7},{6,4},{7,5},{8,10},{9,11},{10,... | collective-permute-start | bytes 3145736 | tf_op jit(solution)/shard_map/ppermute | solution.py:371
  12.5 2.9 %shard_map.132 = f32[2,2,256,256]{3,2,1,0:T(8,128)} custom-call(s32[2]{0:T(128)} %get-tuple-element.93.pick, f32[16,256,256]{2,1,0:T(8,128)} %bitcast.37, f32[16,256,256]{2,1,0:T(8,128)} %bitcast.43), custom_call_target="tpu_custom_call" | custom-call | bytes 2097152 | tf_op jit(solution)/shard_map/pallas_call | solution.py:248
  15.4 2.4 %collective-permute-start.1 = (f32[2,2,256,256]{3,2,1,0:T(8,128)}, f32[2,2,256,256]{3,2,1,0:T(8,128)}, u32[]{:S(2)}, u32[]{:S(2)}) collective-permute-start(f32[2,2,256,256]{3,2,1,0:T(8,128)} %shard_map.132), channel_id=1, source_target_pairs={{0,3},{1,2},{2,1},{3,0},{4,7},{5,6},{6,5},{7,4},{8,11},{9,10},{10,... | collective-permute-start | bytes 3145736 | tf_op jit(solution)/shard_map/ppermute | solution.py:371
  19.6 1.9 %shard_map.145 = f32[512,640]{1,0:T(8,128)} custom-call(f32[1,640]{1,0:T(1,128)} %broadcast_in_dim.7.taps_ref), custom_call_target="tpu_custom_call" | custom-call | tf_op jit(solution)/shard_map/pallas_call | solution.py:273
  21.5 1.7 copy.60
  25.0 1.9 %shard_map.147 = f32[512,640]{1,0:T(8,128)} custom-call(f32[1,640]{1,0:T(1,128)} %broadcast_in_dim.8.taps_ref), custom_call_target="tpu_custom_call" | custom-call | tf_op jit(solution)/shard_map/pallas_call | solution.py:273
  28.1 2.6 %slice.238.across_ref = f32[512,512]{1,0:T(8,128)} slice(f32[512,640]{1,0:T(8,128)} %shard_map.147), slice={[0:512], [20:532]} | slice | bytes 2097152 | tf_op jit(solution)/shard_map/slice | solution.py:286
  31.3 2.9 %fusion = f32[21,512,64]{1,2,0:T(8,128)S(1)} fusion(f32[45,512]{1,0:T(8,128)S(1)} %copy-done.4, f32[45,21]{0,1:T(8,128)S(1)} %copy-done.5, f32[64,45]{0,1:T(8,128)S(1)} %copy-done), kind=kOutput, calls=%fused_computation.1 | convolution fusion | flops 372072960 | bytes 2859972 | tf_op jit(solution)/shard_map/ck,ksl->csl/dot_general | solution.py:365
  34.2 3.3 %copy.62 = f32[21,512,64]{1,0,2:T(8,128)} copy(f32[21,512,64]{1,2,0:T(8,128)S(1)} %fusion) | data formatting | bytes 5505024 | tf_op jit(solution)/shard_map/ck,ksl->csl/dot_general | solution.py:365
  37.5 2.7 %shard_map.133 = f32[2,2,256,256]{3,2,1,0:T(8,128)} custom-call(s32[2]{0:T(128)} %get-tuple-element.60.pick, f32[16,256,256]{2,1,0:T(8,128)} %bitcast.38, f32[16,256,256]{2,1,0:T(8,128)} %bitcast.44), custom_call_target="tpu_custom_call" | custom-call | bytes 2097152 | tf_op jit(solution)/shard_map/pallas_call | solution.py:248
  40.2 2.7 %shard_map.131 = f32[2,2,256,256]{3,2,1,0:T(8,128)} custom-call(s32[2]{0:T(128)} %get-tuple-element.61.pick, f32[16,256,256]{2,1,0:T(8,128)} %bitcast.39, f32[16,256,256]{2,1,0:T(8,128)} %bitcast.45), custom_call_target="tpu_custom_call" | custom-call | bytes 2097152 | tf_op jit(solution)/shard_map/pallas_call | solution.py:248
  46.3 9.6 %shard_map.141 = (f32[512,512]{1,0:T(8,128)}, f32[512,512]{1,0:T(8,128)}) custom-call(s32[2]{0:T(128)} %get-tuple-element.96.pick, s32[2]{0:T(128)} %get-tuple-element.45.coef, s32[4]{0:T(128)} %reshape.86.corner, s32[2]{0:T(128)} %get-tuple-element.44.fill, f32[1,16,256,256]{3,2,1,0:T(8,128)} %exp_ref.3, f32[1,16,256,256]{3,2,1,0:T(8,128)} %var_ref.3, ...), custom_call_target="tpu_custom_call" | custom-call | flops 5368709120 | bytes 5242880 | tf_op jit(solution)/shard_map/pallas_call | solution.py:224
  55.9 9.8 %shard_map.136 = (f32[512,512]{1,0:T(8,128)}, f32[512,512]{1,0:T(8,128)}) custom-call(s32[2]{0:T(128)} %get-tuple-element.58.pick, s32[2]{0:T(128)} %get-tuple-element.97.coef, s32[4]{0:T(128)} %reshape.82.corner, s32[2]{0:T(128)} %get-tuple-element.98.fill, f32[1,16,256,256]{3,2,1,0:T(8,128)} %exp_ref.3, f32[1,16,256,256]{3,2,1,0:T(8,128)} %var_ref.3, ...), custom_call_target="tpu_custom_call" | custom-call | flops 5368709120 | bytes 5242880 | tf_op jit(solution)/shard_map/pallas_call | solution.py:224
  65.7 2.9 %shard_map.135 = f32[2,2,256,256]{3,2,1,0:T(8,128)} custom-call(s32[2]{0:T(128)} %get-tuple-element.59.pick, f32[16,256,256]{2,1,0:T(8,128)} %bitcast.40, f32[16,256,256]{2,1,0:T(8,128)} %bitcast.46), custom_call_target="tpu_custom_call" | custom-call | bytes 2097152 | tf_op jit(solution)/shard_map/pallas_call | solution.py:248
  70.3 1.3 collective-permute-done
  81.2 9.5 %shard_map.142 = (f32[512,512]{1,0:T(8,128)}, f32[512,512]{1,0:T(8,128)}) custom-call(s32[2]{0:T(128)} %iota.44.pick, s32[2]{0:T(128)} %get-tuple-element.51.coef, s32[4]{0:T(128)} %reshape.85.corner, s32[2]{0:T(128)} %get-tuple-element.50.fill, f32[2,2,256,256]{3,2,1,0:T(8,128)} %copy-done.10, f32[2,2,256,256]{3,2,1,0:T(8,128)} %copy-done.10, ...), custom_call_target="tpu_custom_call" | custom-call | flops 5368709120 | bytes 5242880 | tf_op jit(solution)/shard_map/pallas_call | solution.py:224
  91.2 9.5 %shard_map.143 = (f32[512,512]{1,0:T(8,128)}, f32[512,512]{1,0:T(8,128)}) custom-call(s32[2]{0:T(128)} %iota.43.pick, s32[2]{0:T(128)} %get-tuple-element.53.coef, s32[4]{0:T(128)} %reshape.84.corner, s32[2]{0:T(128)} %get-tuple-element.52.fill, f32[2,2,256,256]{3,2,1,0:T(8,128)} %collective-permute-done.4.exp_ref.var_ref, ...), custom_call_target="tpu_custom_call" | custom-call | flops 5368709120 | bytes 5242880 | tf_op jit(solution)/shard_map/pallas_call | solution.py:224
  101.2 9.5 %shard_map.144 = (f32[512,512]{1,0:T(8,128)}, f32[512,512]{1,0:T(8,128)}) custom-call(s32[2]{0:T(128)} %iota.42.pick, s32[2]{0:T(128)} %get-tuple-element.55.coef, s32[4]{0:T(128)} %reshape.83.corner, s32[2]{0:T(128)} %get-tuple-element.54.fill, f32[2,2,256,256]{3,2,1,0:T(8,128)} %collective-permute-done.1.exp_ref.var_ref, ...), custom_call_target="tpu_custom_call" | custom-call | flops 5368709120 | bytes 5242880 | tf_op jit(solution)/shard_map/pallas_call | solution.py:224
  113.5 9.4 %shard_map.137 = (f32[512,512]{1,0:T(8,128)}, f32[512,512]{1,0:T(8,128)}) custom-call(s32[2]{0:T(128)} %iota.41.pick, s32[2]{0:T(128)} %get-tuple-element.63.coef, s32[4]{0:T(128)} %reshape.81.corner, s32[2]{0:T(128)} %get-tuple-element.62.fill, f32[2,2,256,256]{3,2,1,0:T(8,128)} %collective-permute-done.7.exp_ref.var_ref, ...), custom_call_target="tpu_custom_call" | custom-call | flops 5368709120 | bytes 5242880 | tf_op jit(solution)/shard_map/pallas_call | solution.py:224
  123.5 9.5 %shard_map.138 = (f32[512,512]{1,0:T(8,128)}, f32[512,512]{1,0:T(8,128)}) custom-call(s32[2]{0:T(128)} %iota.40.pick, s32[2]{0:T(128)} %get-tuple-element.65.coef, s32[4]{0:T(128)} %reshape.80.corner, s32[2]{0:T(128)} %get-tuple-element.64.fill, f32[2,2,256,256]{3,2,1,0:T(8,128)} %collective-permute-done.5.exp_ref.var_ref, ...), custom_call_target="tpu_custom_call" | custom-call | flops 5368709120 | bytes 5242880 | tf_op jit(solution)/shard_map/pallas_call | solution.py:224
  133.6 9.5 %shard_map.139 = (f32[512,512]{1,0:T(8,128)}, f32[512,512]{1,0:T(8,128)}) custom-call(s32[2]{0:T(128)} %iota.37.pick, s32[2]{0:T(128)} %get-tuple-element.67.coef, s32[4]{0:T(128)} %reshape.79.corner, s32[2]{0:T(128)} %get-tuple-element.66.fill, f32[2,2,256,256]{3,2,1,0:T(8,128)} %collective-permute-done.2.exp_ref.var_ref, ...), custom_call_target="tpu_custom_call" | custom-call | flops 5368709120 | bytes 5242880 | tf_op jit(solution)/shard_map/pallas_call | solution.py:224
  143.1 17.1 %collective-permute-done.9 = f32[512,512]{1,0:T(8,128)} collective-permute-done((f32[512,512]{1,0:T(8,128)}, f32[512,512]{1,0:T(8,128)}, u32[]{:S(2)}, u32[]{:S(2)}) %collective-permute-start.9) | collective-permute-done | bytes 1048608 | tf_op jit(solution)/shard_map/ppermute | solution.py:334
  160.2 2.3 %add_divide_fusion.rows_ref = f32[512,512]{1,0:T(8,128)S(1)} fusion(f32[512,512]{1,0:T(8,128)} %get-tuple-element.40, f32[512,512]{1,0:T(8,128)S(1)} %collective-permute-done.10, f32[512,512]{1,0:T(8,128)} %get-tuple-element.30, f32[512,512]{1,0:T(8,128)} %collective-permute-done.9), kind=kLoop, calls=%fused_computation.3 | loop fusion | flops 1048576 | bytes 5242880 | tf_op jit(solution)/shard_map/div | solution.py:419
  162.7 4.2 %collective-permute-start.11 = (f32[512,20]{1,0:T(8,128)S(1)}, f32[512,20]{1,0:T(8,128)S(1)}, u32[]{:S(2)}, u32[]{:S(2)}) collective-permute-start(f32[512,20]{1,0:T(8,128)S(1)} %get-tuple-element.74), channel_id=1, source_target_pairs={{0,1},{1,2},{2,3},{4,5},{5,6},{6,7},{8,9},{9,10},{10,11},{12,13},{... | collective-permute-start | bytes 122888 | tf_op jit(solution)/shard_map/ppermute | solution.py:334
  167.0 1.9 %collective-permute-start.12 = (f32[512,20]{1,0:T(8,128)S(1)}, f32[512,20]{1,0:T(8,128)S(1)}, u32[]{:S(2)}, u32[]{:S(2)}) collective-permute-start(f32[512,20]{1,0:T(8,128)S(1)} %get-tuple-element.75), channel_id=1, source_target_pairs={{1,0},{2,1},{3,2},{5,4},{6,5},{7,6},{9,8},{10,9},{11,10},{13,12},{... | collective-permute-start | bytes 122888 | tf_op jit(solution)/shard_map/ppermute | solution.py:334
  168.9 1.3 collective-permute-done.11
  170.3 4.4 %collective-permute-done.12 = f32[512,20]{1,0:T(8,128)S(1)} collective-permute-done((f32[512,20]{1,0:T(8,128)S(1)}, f32[512,20]{1,0:T(8,128)S(1)}, u32[]{:S(2)}, u32[]{:S(2)}) %collective-permute-start.12) | collective-permute-done | bytes 40992 | tf_op jit(solution)/shard_map/ppermute | solution.py:334
  174.8 1.5 collective-permute-start.14
  177.2 4.0 %shard_map.146.filtered_ref = f32[512,512]{1,0:T(8,128)} custom-call(f32[512,512]{1,0:T(8,128)} %copy-done.1, f32[512,40]{1,0:T(8,128)} %pad_maximum_fusion.edge_ref, f32[512,512]{1,0:T(8,128)} %slice.227.middle_ref, f32[40,512]{1,0:T(8,128)} %pad_maximum_fusion.2.edges_ref), custom_call_target="tpu_custom_call" | custom-call | flops 805306368 | bytes 2260992 | tf_op jit(solution)/shard_map/pallas_call | solution.py:307
  183.3 4.7 %shard_map.148 = f32[512,512]{1,0:T(8,128)} custom-call(f32[512,512]{1,0:T(8,128)} %shard_map.146.filtered_ref, f32[40,512]{1,0:T(8,128)} %fusion.4.near_ref, f32[40,40]{1,0:T(8,128)} %pad_maximum_fusion.5.corner_ref, f32[512,512]{1,0:T(8,128)} %slice.227.middle_ref, f32[40,512]{1,0:T(8,128)} %pad_maximum_fusion.2.edges_ref, f32[512,512]{1,0:T(8,128)} %slice.238.across_ref, ...), custom_call_target="tpu_custom_call" | custom-call | flops 805306368 | bytes 3397888 | tf_op jit(solution)/shard_map/pallas_call | solution.py:307
  (115 shorter events, 32.4 us)
Async XLA Ops:
  0.6 30.6 %copy-start = (f32[64,45]{0,1:T(8,128)S(1)}, f32[64,45]{0,1:T(8,128)}, u32[]{:S(2)}) copy-start(f32[64,45]{0,1:T(8,128)} %param.14) | copy-start | bytes 34564
  3.4 3.1 %copy-start.6 = (s32[1,16,2]{1,2,0:T(2,128)S(1)}, s32[1,16,2]{1,2,0:T(2,128)}, u32[]{:S(2)}) copy-start(s32[1,16,2]{1,2,0:T(2,128)} %param.16) | copy-start | bytes 388
  3.4 3.1 %copy-start.7 = (s32[1,16]{1,0:T(1,128)S(1)}, s32[1,16]{1,0:T(1,128)}, u32[]{:S(2)}) copy-start(s32[1,16]{1,0:T(1,128)} %param.15) | copy-start | bytes 196
  6.3 73.9 %collective-permute-start.8 = (f32[2,2,256,256]{3,2,1,0:T(8,128)}, f32[2,2,256,256]{3,2,1,0:T(8,128)S(1)}, u32[]{:S(2)}, u32[]{:S(2)}) collective-permute-start(f32[2,2,256,256]{3,2,1,0:T(8,128)} %shard_map.140), channel_id=1, source_target_pairs={{0,1},{1,0},{2,3},{3,2},{4,5},{5,4},{6,7},{7,6},{8,9},{9,8},{10,11... | collective-permute-start | bytes 3145736 | tf_op jit(solution)/shard_map/ppermute | solution.py:371
  7.0 61.6 %collective-permute-start.6 = (s32[2,2,4]{2,1,0:T(2,128)S(1)}, s32[2,2,4]{2,1,0:T(2,128)S(1)}, u32[]{:S(2)}, u32[]{:S(2)}) collective-permute-start(s32[2,2,4]{2,1,0:T(2,128)S(1)} %bitcast.63), channel_id=1, source_target_pairs={{0,1},{1,0},{2,3},{3,2},{4,5},{5,4},{6,7},{7,6},{8,9},{9,8},{10,11... | collective-permute-start | bytes 200 | tf_op jit(solution)/shard_map/ppermute | solution.py:371
  10.2 68.7 %collective-permute-start.4 = (f32[2,2,256,256]{3,2,1,0:T(8,128)}, f32[2,2,256,256]{3,2,1,0:T(8,128)}, u32[]{:S(2)}, u32[]{:S(2)}) collective-permute-start(f32[2,2,256,256]{3,2,1,0:T(8,128)} %shard_map.134), channel_id=1, source_target_pairs={{0,2},{1,3},{2,0},{3,1},{4,6},{5,7},{6,4},{7,5},{8,10},{9,11},{10,... | collective-permute-start | bytes 3145736 | tf_op jit(solution)/shard_map/ppermute | solution.py:371
  12.5 56.8 %collective-permute-start.3 = (s32[2,2,4]{2,1,0:T(2,128)S(1)}, s32[2,2,4]{2,1,0:T(2,128)S(1)}, u32[]{:S(2)}, u32[]{:S(2)}) collective-permute-start(s32[2,2,4]{2,1,0:T(2,128)S(1)} %bitcast.62), channel_id=1, source_target_pairs={{0,2},{1,3},{2,0},{3,1},{4,6},{5,7},{6,4},{7,5},{8,10},{9,11},{10,... | collective-permute-start | bytes 200 | tf_op jit(solution)/shard_map/ppermute | solution.py:371
  12.5 6.5 %copy-start.8 = (f32[41]{0:T(128)S(1)}, f32[41]{0:T(128)}, u32[]{:S(2)}) copy-start(f32[41]{0:T(128)} %param.19) | copy-start | bytes 496
  15.4 63.5 %collective-permute-start.1 = (f32[2,2,256,256]{3,2,1,0:T(8,128)}, f32[2,2,256,256]{3,2,1,0:T(8,128)}, u32[]{:S(2)}, u32[]{:S(2)}) collective-permute-start(f32[2,2,256,256]{3,2,1,0:T(8,128)} %shard_map.132), channel_id=1, source_target_pairs={{0,3},{1,2},{2,1},{3,0},{4,7},{5,6},{6,5},{7,4},{8,11},{9,10},{10,... | collective-permute-start | bytes 3145736 | tf_op jit(solution)/shard_map/ppermute | solution.py:371
  21.5 2.8 %copy-start.9 = (f32[41]{0:T(128)S(1)}, f32[41]{0:T(128)}, u32[]{:S(2)}) copy-start(f32[41]{0:T(128)} %param.18) | copy-start | bytes 496
  24.9 6.3 %copy-start.4 = (f32[45,512]{1,0:T(8,128)S(1)}, f32[45,512]{1,0:T(8,128)}, u32[]{:S(2)}) copy-start(f32[45,512]{1,0:T(8,128)} %constant.60.clone) | copy-start | bytes 276484
  25.0 6.3 %copy-start.5 = (f32[45,21]{0,1:T(8,128)S(1)}, f32[45,21]{0,1:T(8,128)}, u32[]{:S(2)}) copy-start(f32[45,21]{0,1:T(8,128)} %constant.59.clone) | copy-start | bytes 11344
  65.7 13.2 %copy-start.3 = (f32[2,2,256,256]{3,2,1,0:T(8,128)S(1)}, f32[2,2,256,256]{3,2,1,0:T(8,128)}, u32[]{:S(2)}) copy-start(f32[2,2,256,256]{3,2,1,0:T(8,128)} %shard_map.133) | copy-start | bytes 3145732
  65.7 13.6 %copy-start.2 = (f32[2,2,256,256]{3,2,1,0:T(8,128)S(1)}, f32[2,2,256,256]{3,2,1,0:T(8,128)}, u32[]{:S(2)}) copy-start(f32[2,2,256,256]{3,2,1,0:T(8,128)} %shard_map.131) | copy-start | bytes 3145732
  68.6 3.0 %collective-permute-start = (s32[2,2,4]{2,1,0:T(2,128)S(1)}, s32[2,2,4]{2,1,0:T(2,128)S(1)}, u32[]{:S(2)}, u32[]{:S(2)}) collective-permute-start(s32[2,2,4]{2,1,0:T(2,128)S(1)} %bitcast.64), channel_id=1, source_target_pairs={{0,3},{1,2},{2,1},{3,0},{4,7},{5,6},{6,5},{7,4},{8,11},{9,10},{10,... | collective-permute-start | bytes 200 | tf_op jit(solution)/shard_map/ppermute | solution.py:371
  69.4 43.7 %collective-permute-start.7 = (f32[2,2,256,256]{3,2,1,0:T(8,128)}, f32[2,2,256,256]{3,2,1,0:T(8,128)}, u32[]{:S(2)}, u32[]{:S(2)}) collective-permute-start(f32[2,2,256,256]{3,2,1,0:T(8,128)} %shard_map.135), channel_id=1, source_target_pairs={{0,1},{1,0},{2,3},{3,2},{4,5},{5,4},{6,7},{7,6},{8,9},{9,8},{10,11... | collective-permute-start | bytes 3145736 | tf_op jit(solution)/shard_map/ppermute | solution.py:371
  78.9 44.1 %collective-permute-start.5 = (f32[2,2,256,256]{3,2,1,0:T(8,128)S(1)}, f32[2,2,256,256]{3,2,1,0:T(8,128)}, u32[]{:S(2)}, u32[]{:S(2)}) collective-permute-start(f32[2,2,256,256]{3,2,1,0:T(8,128)S(1)} %copy-done.3), channel_id=1, source_target_pairs={{0,2},{1,3},{2,0},{3,1},{4,6},{5,7},{6,4},{7,5},{8,10},{9,11},{10,... | collective-permute-start | bytes 3145736 | tf_op jit(solution)/shard_map/ppermute | solution.py:371
  79.3 53.7 %collective-permute-start.2 = (f32[2,2,256,256]{3,2,1,0:T(8,128)S(1)}, f32[2,2,256,256]{3,2,1,0:T(8,128)}, u32[]{:S(2)}, u32[]{:S(2)}) collective-permute-start(f32[2,2,256,256]{3,2,1,0:T(8,128)S(1)} %copy-done.2), channel_id=1, source_target_pairs={{0,3},{1,2},{2,1},{3,0},{4,7},{5,6},{6,5},{7,4},{8,11},{9,10},{10,... | collective-permute-start | bytes 3145736 | tf_op jit(solution)/shard_map/ppermute | solution.py:371
  80.2 1.0 copy-start.10
  110.7 32.4 %collective-permute-start.10 = (f32[512,512]{1,0:T(8,128)}, f32[512,512]{1,0:T(8,128)S(1)}, u32[]{:S(2)}, u32[]{:S(2)}) collective-permute-start(f32[512,512]{1,0:T(8,128)} %get-tuple-element.41), channel_id=1, source_target_pairs={{0,4},{1,5},{2,6},{3,7},{4,8},{5,9},{6,10},{7,11},{8,12},{9,13},{1... | collective-permute-start | bytes 3145736 | tf_op jit(solution)/shard_map/ppermute | solution.py:334
  111.9 48.4 %collective-permute-start.9 = (f32[512,512]{1,0:T(8,128)}, f32[512,512]{1,0:T(8,128)}, u32[]{:S(2)}, u32[]{:S(2)}) collective-permute-start(f32[512,512]{1,0:T(8,128)} %get-tuple-element.39), channel_id=1, source_target_pairs={{0,4},{1,5},{2,6},{3,7},{4,8},{5,9},{6,10},{7,11},{8,12},{9,13},{1... | collective-permute-start | bytes 3145736 | tf_op jit(solution)/shard_map/ppermute | solution.py:334
  162.6 14.6 %copy-start.1 = (f32[512,512]{1,0:T(8,128)}, f32[512,512]{1,0:T(8,128)S(1)}, u32[]{:S(2)}) copy-start(f32[512,512]{1,0:T(8,128)S(1)} %add_divide_fusion.rows_ref) | copy-start | bytes 3145732
  162.7 7.5 %collective-permute-start.11 = (f32[512,20]{1,0:T(8,128)S(1)}, f32[512,20]{1,0:T(8,128)S(1)}, u32[]{:S(2)}, u32[]{:S(2)}) collective-permute-start(f32[512,20]{1,0:T(8,128)S(1)} %get-tuple-element.74), channel_id=1, source_target_pairs={{0,1},{1,2},{2,3},{4,5},{5,6},{6,7},{8,9},{9,10},{10,11},{12,13},{... | collective-permute-start | bytes 122888 | tf_op jit(solution)/shard_map/ppermute | solution.py:334
  167.0 7.7 %collective-permute-start.12 = (f32[512,20]{1,0:T(8,128)S(1)}, f32[512,20]{1,0:T(8,128)S(1)}, u32[]{:S(2)}, u32[]{:S(2)}) collective-permute-start(f32[512,20]{1,0:T(8,128)S(1)} %get-tuple-element.75), channel_id=1, source_target_pairs={{1,0},{2,1},{3,2},{5,4},{6,5},{7,6},{9,8},{10,9},{11,10},{13,12},{... | collective-permute-start | bytes 122888 | tf_op jit(solution)/shard_map/ppermute | solution.py:334
  174.8 6.4 %collective-permute-start.14 = (f32[20,552]{1,0:T(8,128)S(1)}, f32[20,552]{1,0:T(8,128)S(1)}, u32[]{:S(2)}, u32[]{:S(2)}) collective-permute-start(f32[20,552]{1,0:T(8,128)S(1)} %pad_maximum_fusion.4), channel_id=1, source_target_pairs={{0,28},{1,29},{2,30},{3,31},{4,0},{5,1},{6,2},{7,3},{8,4},{9,5},{1... | collective-permute-start | bytes 132488 | tf_op jit(solution)/shard_map/ppermute | solution.py:334
  176.3 5.8 %collective-permute-start.13 = (f32[20,552]{1,0:T(8,128)S(1)}, f32[20,552]{1,0:T(8,128)S(1)}, u32[]{:S(2)}, u32[]{:S(2)}) collective-permute-start(f32[20,552]{1,0:T(8,128)S(1)} %pad_maximum_fusion.3), channel_id=1, source_target_pairs={{0,4},{1,5},{2,6},{3,7},{4,8},{5,9},{6,10},{7,11},{8,12},{9,13},{1... | collective-permute-start | bytes 132488 | tf_op jit(solution)/shard_map/ppermute | solution.py:334
